TPU v7x, 768 devices: a whole 4x8x12 slice. The times are simulated.
768 devices in a mesh: rep: 16 (over x, z_hi), grp: 48 (over z_lo, y, core).
Axes of the slice: x: 4, y: 8, z: 12 (z_hi: 4, z_lo: 3; z = z_hi * 3 + z_lo), core: 2. Of those that a mesh axis runs over, the one named last changes fastest.
Arguments:
- tokens: bfloat16 [196608, 4608], P(('rep', 'grp')), may hold values from -24 to 24
- key_cotangent: bfloat16 [196608, 512], P(('rep', 'grp')), may hold values from -0.03125 to 0.03125
- weight_codes: bfloat16 [144, 128, 128], P('grp'), may hold values from -6 to 6
- block_scales: bfloat16 [144, 1, 128], P('grp'), may hold values from 0.0059814453 to 0.023925781
- master_weight: float32 [4608, 512], P(('rep', 'grp')), may hold values from -3 to 3
- first_moment: float32 [4608, 512], P(('rep', 'grp')), may hold values from -6 to 6
- second_moment: float32 [4608, 512], P(('rep', 'grp')), may hold values from 0.25 to 4
Outputs:
- projected: bfloat16 [196608, 512], P(('rep', 'grp'))
- new_first: float32 [4608, 512], P(('rep', 'grp'))
- new_second: float32 [4608, 512], P(('rep', 'grp'))
- new_weight: float32 [4608, 512], P(('rep', 'grp'))
All inputs are finite; a program needn't handle non-finite values.
Results may differ from a plain program's by a relative error of at most 0.0049.
Values may be sent and summed in bfloat16 or wider, within the bound.
No kernel may reach another device: no remote copies, remote signals or barrier semaphores. Data moves between devices by JAX's collectives and lax.ppermute only.
A program may use at most 64 MiB of HBM per device.

v0:
```python
import jax
import jax.numpy as jnp
from jax import lax
from jax.sharding import PartitionSpec as P

BETA_ONE = 0.9
BETA_TWO = 0.99
STEP_SIZE = 0.5
EPSILON = 1e-08
CORRECT_ONE = 1.0 - 0.9**20
CORRECT_TWO = 1.0 - 0.99**20


def local(
    tokens, key_cotangent, weight_codes, block_scales, master_weight, first_moment, second_moment
):
    rows_here = tokens.shape[0]
    width = tokens.shape[1]
    block = weight_codes.shape[1]
    columns = key_cotangent.shape[1]
    col_blocks = columns // block
    row_blocks = width // block
    blocked = tokens.reshape(rows_here, row_blocks, block)
    empty = jnp.zeros((rows_here, col_blocks, block), jnp.float32)
    group_count = lax.axis_size("grp")
    replica_count = lax.axis_size("rep")
    scaled = (
        lax.all_gather(weight_codes, "grp", axis=0, tiled=True).astype(jnp.float32)
        * lax.all_gather(block_scales, "grp", axis=0, tiled=True).astype(jnp.float32)
    ).astype(jnp.bfloat16)
    count = scaled.shape[0]
    group_size = max((d for d in range(1, min(count, 12) + 1) if count % d == 0))
    grouped = scaled.reshape(count // group_size, group_size, block, block)
    offsets = jnp.arange(count // group_size, dtype=jnp.int32) * group_size

    def one_group(acc, pair):
        tiles, offset = pair
        indices = offset + jnp.arange(group_size, dtype=jnp.int32)
        row_ids = indices // col_blocks
        col_ids = indices % col_blocks
        window = jnp.take(blocked, row_ids, axis=1)
        partial_value = jnp.einsum(
            "rkb,kbc->rkc", window, tiles, preferred_element_type=jnp.float32
        )
        placing = (col_ids[:, None] == jnp.arange(col_blocks, dtype=jnp.int32)[None, :]).astype(
            jnp.float32
        )
        placed = jnp.einsum("rkc,kj->rjc", partial_value, placing, precision=lax.Precision.HIGHEST)
        return (acc + placed, None)

    result, _ = lax.scan(one_group, empty, (grouped, offsets))
    projected = result.reshape(rows_here, columns).astype(jnp.bfloat16)
    term = lax.dot_general(
        tokens, key_cotangent, (((0,), (0,)), ((), ())), preferred_element_type=jnp.float32
    )
    rounded = term.astype(jnp.bfloat16)
    share = width // (group_count * replica_count)
    widened = lax.optimization_barrier(rounded).astype(jnp.float32)
    ordered = widened.reshape(replica_count, group_count, share, columns)
    reduced = lax.psum_scatter(
        ordered.astype(jnp.bfloat16), "rep", scatter_dimension=0, tiled=True
    ).astype(jnp.float32)
    arrived = lax.all_to_all(
        reduced.reshape(group_count, share, columns).astype(jnp.bfloat16),
        "grp",
        split_axis=0,
        concat_axis=0,
        tiled=True,
    ).astype(jnp.float32)
    gradient = jnp.sum(arrived, axis=0)
    new_first = BETA_ONE * first_moment + (1.0 - BETA_ONE) * gradient
    new_second = BETA_TWO * second_moment + (1.0 - BETA_TWO) * gradient * gradient
    update = new_first / CORRECT_ONE / (jnp.sqrt(new_second / CORRECT_TWO) + EPSILON)
    new_weight = master_weight - STEP_SIZE * update
    return (projected, new_first, new_second, new_weight)


def solution(mesh):
    placed = (
        P(("rep", "grp"), None),
        P(("rep", "grp"), None),
        P("grp", None, None),
        P("grp", None, None),
        P(("rep", "grp"), None),
        P(("rep", "grp"), None),
        P(("rep", "grp"), None),
    )
    return jax.shard_map(
        local,
        mesh=mesh,
        in_specs=placed,
        out_specs=(
            P(("rep", "grp"), None),
            P(("rep", "grp"), None),
            P(("rep", "grp"), None),
            P(("rep", "grp"), None),
        ),
        check_vma=False,
    )
```

profile of v0, /device:TPU:205, one launch (start us, length us, event | category | flops | bytes accessed | tf_op | source)
XLA Modules:
  0.0 430.3 jit_solution(2316034864434961121)
XLA Ops:
  9.0 5.3 %convolution_convert_fusion = bf16[4608,512]{1,0:T(8,128)(2,1)} fusion(bf16[256,4608]{1,0:T(8,128)(2,1)} %param.9, bf16[256,512]{1,0:T(8,128)(2,1)S(1)} %copy-done), kind=kOutput, calls=%fused_computation.31 | convolution fusion | flops 1210318848 | bytes 7340032 | tf_op jit(solution)/shard_map/dot_general | solution.py:53
  14.2 8.7 %convert_element_type.35 = bf16[16,48,6,512]{3,2,1,0:T(8,128)(2,1)} reshape(bf16[4608,512]{1,0:T(8,128)(2,1)} %convolution_convert_fusion) | data formatting | bytes 9437184 | tf_op jit(solution)/shard_map/convert_element_type | solution.py:61
  24.6 2.5 copy.15
  27.1 67.5 %all_gather.7 = bf16[144,1,128]{2,1,0:T(2,128)(2,1)S(1)} all-gather(bf16[3,1,128]{2,1,0:T(2,128)(2,1)S(1)} %copy.14), channel_id=1, replica_groups=mesh['rep'=16,'grp'=48] {'grp'}, dimensions={0}, use_global_device_ids=true | all-gather | bytes 37632 | tf_op jit(solution)/shard_map/all_gather | solution.py:29
  94.6 4.3 copy.17
  98.9 169.3 %all-gather.2.cloned.1.call-done = bf16[144,128,128]{2,1,0:T(8,128)(2,1)} async-done(((bf16[3,128,128]{2,1,0:T(8,128)(2,1)}), bf16[144,128,128]{2,1,0:T(8,128)(2,1)}) %all-gather.2.cloned.1.call-update) | async-done | bytes 4718608 | tf_op jit(solution)/shard_map/all_gather | solution.py:28
  268.2 6.6 %multiply_convert_fusion = bf16[144,128,128]{2,1,0:T(8,128)(2,1)} fusion(bf16[144,128,128]{2,1,0:T(8,128)(2,1)} %all-gather.2.cloned.1.call-done, f32[144,128]{1,0:T(8,128)S(1)} %bitcast.50), kind=kLoop, calls=%fused_computation.30 | loop fusion | flops 7077888 | bytes 9510912 | tf_op jit(solution)/shard_map/convert_element_type | solution.py:30
  274.8 12.9 %all-to-all-start = ((bf16[48,6,512]{2,1,0:T(8,128)(2,1)}), bf16[48,6,512]{2,1,0:T(8,128)(2,1)S(1)}, u32[]{:S(2)}, u32[]{:S(2)}) async-start(bf16[48,6,512]{2,1,0:T(8,128)(2,1)} %bitcast.49), calls=%async_computation.1 | async-start | bytes 786432 | tf_op jit(solution)/shard_map/all_to_all | solution.py:63
  287.8 133.5 %while.13 = (s32[]{:T(128)}, f32[256,4,128]{2,1,0:T(4,128)S(1)}, s32[12]{0:T(128)S(1)}, bf16[12,12,128,128]{3,2,1,0:T(8,128)(2,1)}, bf16[256,36,128]{2,0,1:T(8,128)(2,1)}, /*index=5*/s32[]{:T(128)}, s32[]{:T(128)}) while((s32[]{:T(128)}, f32[256,4,128]{2,1,0:T(4,128)S(1)}, s32[12]{0:T(128)S(1)}, ...), condition=%wide.region_1.2_spmd.clone, body=%wide.region_0.1_spmd.clone.sunk | while | flops 120194736 | bytes 10097027 | solution.py:51
  290.4 2.4 gather_fusion
  292.7 2.6 convolution_bitcast_fusion.3
  301.5 2.4 gather_fusion
  303.8 2.6 convolution_bitcast_fusion.3
  312.6 2.4 gather_fusion
  315.0 2.6 convolution_bitcast_fusion.3
  323.7 2.4 gather_fusion
  326.1 2.6 convolution_bitcast_fusion.3
  334.8 2.4 gather_fusion
  337.2 2.6 convolution_bitcast_fusion.3
  346.0 2.4 gather_fusion
  348.3 2.6 convolution_bitcast_fusion.3
  357.1 2.4 gather_fusion
  359.5 2.6 convolution_bitcast_fusion.3
  368.2 2.4 gather_fusion
  370.6 2.6 convolution_bitcast_fusion.3
  379.3 2.4 gather_fusion
  381.7 2.6 convolution_bitcast_fusion.3
  390.5 2.4 gather_fusion
  392.8 2.6 convolution_bitcast_fusion.3
  404.0 2.6 convolution_bitcast_fusion.3
  412.7 2.4 gather_fusion
  415.1 2.6 convolution_bitcast_fusion.3
  (111 shorter events, 79.8 us)
Async XLA Ops:
  8.0 1.0 copy-start
  8.0 260.2 %all-gather.2.cloned.1.call-start = ((), (), s32[]{:S(2)}) async-start(), calls=%async_computation.2 | async-start | bytes 4816896 | tf_op jit(solution)/shard_map/all_gather | solution.py:28
  8.7 266.0 %reduce-scatter.2.cloned.1.call-start = ((), (), s32[]{:S(2)}) async-start(), calls=%async_computation.3 | async-start | bytes 6684672 | tf_op jit(solution)/shard_map/reduce_scatter | solution.py:60
  22.9 1.7 copy-start.1
  22.9 4.2 copy-start.5
  274.8 147.3 %all-to-all-start = ((bf16[48,6,512]{2,1,0:T(8,128)(2,1)}), bf16[48,6,512]{2,1,0:T(8,128)(2,1)S(1)}, u32[]{:S(2)}, u32[]{:S(2)}) async-start(bf16[48,6,512]{2,1,0:T(8,128)(2,1)} %bitcast.49), calls=%async_computation.1 | async-start | bytes 786432 | tf_op jit(solution)/shard_map/all_to_all | solution.py:63
  287.7 134.5 %copy-start.2 = (f32[6,512]{1,0:T(8,128)S(1)}, f32[6,512]{1,0:T(8,128)}, u32[]{:S(2)}) copy-start(f32[6,512]{1,0:T(8,128)} %param.13) | copy-start | bytes 36868
  287.7 134.5 %copy-start.3 = (f32[6,512]{1,0:T(8,128)S(1)}, f32[6,512]{1,0:T(8,128)}, u32[]{:S(2)}) copy-start(f32[6,512]{1,0:T(8,128)} %param.15) | copy-start | bytes 36868
  287.7 134.5 %copy-start.4 = (f32[6,512]{1,0:T(8,128)S(1)}, f32[6,512]{1,0:T(8,128)}, u32[]{:S(2)}) copy-start(f32[6,512]{1,0:T(8,128)} %param.14) | copy-start | bytes 36868
Sparse Core Ops, SparseCore 0:
  11.2 256.8 all-gather.1
Sparse Core Ops, SparseCore 1:
  23.0 150.6 reduce-scatter.1
where the time goes:
time: 432 us; the launch traced here: 430 us
  waiting for transfers between devices  170 us (39%)
  local copies, waits for them, and re-layouts  79.2 us (18%)
  blocking collectives  67.5 us (16%)
  matrix products  53.2 us (12%)
  other arithmetic  31.3 us (7%)
  between operations  15.6 us (4%)
  starting transfers between devices  13 us (3%)
    all_gather x1, waiting for transfers between devices, local(): lax.all_gather(weight_codes, 'grp', axis=0, tiled=True).astype(jnp.float32)  169 us
    all_gather x1, blocking collectives, local(): lax.all_gather(block_scales, 'grp', axis=0, tiled=True).astype(jnp.float32)  67.5 us
    dot_general x12, matrix products, one_group(): jnp.einsum('rkb,kbc->rkc', window, tiles, preferred_element_type=jnp.floa...  31.3 us
    gather x12, local copies, waits for them, and re-layouts, one_group(): window = jnp.take(blocked, row_ids, axis=1)  28.4 us
    transpose x12, local copies, waits for them, and re-layouts, one_group(): jnp.einsum('rkb,kbc->rkc', window, tiles, preferred_element_type=jnp.floa...  25.8 us
    dot_general x12, matrix products, one_group(): jnp.einsum('rkc,kj->rjc', partial_value, placing, precision=lax.Precision...  16.6 us
    all_to_all x1, starting transfers between devices, local(): lax.all_to_all(reduced.reshape(group_count, share, columns).astype(jnp.bf...  12.9 us
    unnamed x16, local copies, waits for them, and re-layouts  9.35 us
  transfers between devices with their start and end apart: 3, of which 1 were waited for; matrix products, arithmetic and copies ran while one was open for 37% of the time, Pallas kernels for 0%

commit v1 on v0

v1 whole, which is shorter than its diff:
```python
import jax
import jax.numpy as jnp
from jax import lax
from jax.experimental import pallas as pl
from jax.experimental.pallas import tpu as pltpu
from jax.sharding import Mesh, PartitionSpec as P

BETA_ONE = 0.9
BETA_TWO = 0.99
STEP_SIZE = 0.5
EPSILON = 1e-08
CORRECT_ONE = 1.0 - 0.9**20
CORRECT_TWO = 1.0 - 0.99**20
NX, NZH, NZL, NY, NC = 4, 4, 3, 8, 2
AXES = ("x", "zh", "zl", "y", "c")
BF = jnp.bfloat16
F32 = jnp.float32
SLABS = 6


def project_kernel(tokens_ref, tiles_ref, out_ref, weights, sems):
    blk = tiles_ref.shape[-1]
    cbs = out_ref.shape[1] // blk
    rows = weights.shape[0] // SLABS
    per_slab = (rows // blk) * cbs

    def slab(s):
        return weights.at[pl.ds(s * rows, rows)]

    for s in range(SLABS):
        for t in range(s * per_slab, (s + 1) * per_slab):
            owner, i = divmod(t, 3)
            z, q = divmod(owner, NY * NC)
            pltpu.make_async_copy(
                tiles_ref.at[q, z * 3 + i],
                weights.at[pl.ds(t // cbs * blk, blk), pl.ds(t % cbs * blk, blk)],
                sems.at[s],
            ).start()
    total = None
    for s in range(SLABS):
        pltpu.make_async_copy(slab(s), slab(s), sems.at[s]).wait()
        part = jnp.dot(tokens_ref[:, s * rows : (s + 1) * rows], slab(s)[...], preferred_element_type=F32)
        total = part if total is None else total + part
    out_ref[...] = total.astype(out_ref.dtype)


def project(tokens, tiles, columns):
    rows, width = tokens.shape
    return pl.pallas_call(
        project_kernel,
        out_shape=jax.ShapeDtypeStruct((rows, columns), BF),
        in_specs=[pl.BlockSpec(memory_space=pltpu.VMEM), pl.BlockSpec(memory_space=pl.ANY)],
        out_specs=pl.BlockSpec(memory_space=pltpu.VMEM),
        scratch_shapes=[pltpu.VMEM((width, columns), BF), pltpu.SemaphoreType.DMA((SLABS,))],
        compiler_params=pltpu.CompilerParams(vmem_limit_bytes=24 * 2**20),
        cost_estimate=pl.CostEstimate(
            flops=2 * rows * width * columns, bytes_accessed=2 * (rows * width + width * columns), transcendentals=0
        ),
    )(tokens, tiles)


def dot_t(a, b):
    return lax.dot_general(a, b, (((0,), (0,)), ((), ())), preferred_element_type=F32)


def local(tokens, cot, codes, scales, master, first, second):
    width, columns = tokens.shape[1], cot.shape[1]
    x, zl, c = (lax.axis_index(a).astype(jnp.uint32) for a in ("x", "zl", "c"))

    w = (codes.astype(F32) * scales.astype(F32)).astype(BF)
    nz = NZH * NZL
    below = lax.ppermute(w, ("zh", "zl"), [(i, (i + 1) % nz) for i in range(nz)])
    above = lax.ppermute(w, ("zh", "zl"), [(i, (i - 1) % nz) for i in range(nz)])
    cyc = jnp.concatenate([w, above, below, w, above])
    ordered = lax.dynamic_slice_in_dim(cyc, jnp.where(zl == 0, 0, 3 - zl) * w.shape[0], 3 * w.shape[0])
    tiles = lax.all_gather(ordered, ("y", "c"), axis=0)

    chunk, half = width // NX, columns // 2
    swap = [(0, 1), (1, 0)]
    mine_on, their_on = x + 1 + 2 * c, x + 3 - 2 * c

    def part(j):
        return lax.dynamic_slice_in_dim(tokens, (j & (NX - 1)) * chunk, chunk, axis=1)

    theirs = lax.ppermute(jnp.stack([part(x + 2), part(their_on), part(x)]), "c", swap)
    cot_theirs = lax.ppermute(cot, "c", swap)
    near = [lax.dynamic_slice_in_dim(k, c * half, half, axis=1) for k in (cot, cot_theirs)]
    far = [lax.dynamic_slice_in_dim(k, (1 - c) * half, half, axis=1) for k in (cot, cot_theirs)]

    def term(k, j, cots):
        return dot_t(part(j), cots[0]) + dot_t(theirs[k], cots[1])

    straight = [(2 * i + d, 2 * ((i + 1 - 2 * d) % NX) + d) for i in range(NX) for d in range(2)]
    crossed = [(2 * i + d, 2 * ((i + 1 - 2 * d) % NX) + 1 - d) for i in range(NX) for d in range(2)]
    two_on = lax.ppermute(term(0, x + 2, near).astype(BF), ("x", "c"), straight)
    one_far = lax.ppermute(term(1, mine_on, far).astype(BF), ("x", "c"), crossed)
    one_near = (term(1, mine_on, near) + two_on.astype(F32)).astype(BF)
    one_near = lax.ppermute(one_near, ("x", "c"), straight)
    summed = (term(2, x, near) + one_far.astype(F32) + one_near.astype(F32)).astype(BF)

    rows = chunk // (nz * NY)
    by_y = summed.reshape(nz, NY, rows, half).transpose(1, 0, 2, 3)
    by_y = lax.all_to_all(by_y, "y", 0, 0, tiled=True)
    by_z = jnp.sum(by_y.astype(F32), axis=0).astype(BF).reshape(nz * NC, rows // NC, half)
    by_z = lax.all_to_all(by_z, ("zh", "zl", "c"), 0, 0, tiled=True)
    gradient = jnp.sum(by_z.astype(F32).reshape(nz, NC, rows // NC, half), axis=0)
    gradient = gradient.transpose(1, 0, 2).reshape(rows // NC, columns)

    projected = project(tokens, tiles, columns)
    new_first = BETA_ONE * first + (1.0 - BETA_ONE) * gradient
    new_second = BETA_TWO * second + (1.0 - BETA_TWO) * gradient * gradient
    update = new_first / CORRECT_ONE / (jnp.sqrt(new_second / CORRECT_TWO) + EPSILON)
    new_weight = master - STEP_SIZE * update
    return projected, new_first, new_second, new_weight


def solution(mesh):
    fine = Mesh(mesh.devices.reshape(NX, NZH, NZL, NY, NC), AXES)
    rows = P(AXES, None)
    tiles = P(("zl", "y", "c"), None, None)
    return jax.shard_map(
        local,
        mesh=fine,
        in_specs=(rows, rows, tiles, tiles, rows, rows, rows),
        out_specs=(rows, rows, rows, rows),
        check_vma=False,
    )
```

time: 432 us -> 132 us (0.31)
  the two profiles are of different devices: /device:TPU:205 before, /device:TPU:1 now
where the time goes in v1:
time: 132 us; the launch traced here: 131 us
  blocking collectives  44.8 us (34%)
  starting transfers between devices  35.3 us (27%)
  waiting for transfers between devices  14.6 us (11%)
  between operations  14.3 us (11%)
  matrix products  9.02 us (7%)
  local copies, waits for them, and re-layouts  6.06 us (5%)
  other arithmetic  3.86 us (3%)
  Pallas kernels  3.33 us (3%)
    all_to_all x1, blocking collectives, local(): by_y = lax.all_to_all(by_y, 'y', 0, 0, tiled=True)  25.8 us
    all_to_all x1, blocking collectives, local(): by_z = lax.all_to_all(by_z, ('zh', 'zl', 'c'), 0, 0, tiled=True)  19 us
    ppermute x1, starting transfers between devices, local(): lax.ppermute(w, ('zh', 'zl'), [(i, (i - 1) % nz) for i in range(nz)])  15.1 us
    dot_general x8, matrix products, dot_t(): lax.dot_general(a, b, (((0,), (0,)), ((), ())), preferred_element_type=F32)  9.02 us
    ppermute x1, waiting for transfers between devices, local(): one_near = lax.ppermute(one_near, ('x', 'c'), straight)  5.48 us
    ppermute x1, starting transfers between devices, local(): one_near = lax.ppermute(one_near, ('x', 'c'), straight)  5.3 us
    ppermute x1, waiting for transfers between devices, local(): lax.ppermute(w, ('zh', 'zl'), [(i, (i + 1) % nz) for i in range(nz)])  4.59 us
    ppermute x1, starting transfers between devices, local(): two_on = lax.ppermute(term(0, x + 2, near).astype(BF), ('x', 'c'), straight)  4.38 us
  transfers between devices with their start and end apart: 8, of which 5 were waited for; matrix products, arithmetic and copies ran while one was open for 11% of the time, Pallas kernels for 0%

profile of v1, /device:TPU:1, one launch (start us, length us, event | category | flops | bytes accessed | tf_op | source)
XLA Modules:
  0.0 131.3 jit_solution(4526418383790524426)
XLA Ops:
  7.2 0.7 bitcast_convert_fusion
  7.9 0.9 constant_dynamic-update-slice_fusion.4
  8.8 15.1 %collective-permute-start = (bf16[3,128,128]{2,1,0:T(8,128)(2,1)S(1)}, bf16[3,128,128]{2,1,0:T(8,128)(2,1)S(1)}, u32[]{:S(2)}, u32[]{:S(2)}) collective-permute-start(bf16[3,128,128]{2,1,0:T(8,128)(2,1)S(1)} %get-tuple-element.8), channel_id=1, source_target_pairs={{0,176},{16,0},{32,16},{48,32},{64,48},{80,64},{96,80},{112,96},{1... | collective-permute-start | bytes 294920 | tf_op jit(solution)/shard_map/ppermute | solution.py:73
  24.0 1.9 %collective-permute-start.1 = (bf16[3,128,128]{2,1,0:T(8,128)(2,1)S(1)}, bf16[3,128,128]{2,1,0:T(8,128)(2,1)S(1)}, u32[]{:S(2)}, u32[]{:S(2)}) collective-permute-start(bf16[3,128,128]{2,1,0:T(8,128)(2,1)S(1)} %get-tuple-element.8), channel_id=1, source_target_pairs={{0,16},{16,32},{32,48},{48,64},{64,80},{80,96},{96,112},{112,128},... | collective-permute-start | bytes 294920 | tf_op jit(solution)/shard_map/ppermute | solution.py:72
  25.9 4.6 %collective-permute-done.1 = bf16[3,128,128]{2,1,0:T(8,128)(2,1)S(1)} collective-permute-done((bf16[3,128,128]{2,1,0:T(8,128)(2,1)S(1)}, bf16[3,128,128]{2,1,0:T(8,128)(2,1)S(1)}, u32[]{:S(2)}, u32[]{:S(2)}) %collective-permute-start.1) | collective-permute-done | bytes 98336 | tf_op jit(solution)/shard_map/ppermute | solution.py:72
  30.6 0.8 constant_dynamic-slice_fusion
  31.4 1.6 %dynamic-slice_bitcast_fusion.1 = (bf16[1,256,1152]{2,1,0:T(8,128)(2,1)S(1)}, bf16[1,256,1152]{2,1,0:T(8,128)(2,1)S(1)}, bf16[1,256,1152]{2,1,0:T(8,128)(2,1)S(1)}) fusion(bf16[256,4608]{1,0:T(8,128)(2,1)} %tokens_ref.1, u32[]{:T(128)S(6)} %mul.85, u32[]{:T(128)S(6)} %mul.83, u32[]{:T(128)S(6)} %mul.87), kind=kLoop, calls=%fused_computation.22 | loop fusion | bytes 3538956 | tf_op jit(solution)/shard_map/stack | solution.py:85
  33.0 1.5 %pad_maximum_fusion = bf16[3,256,1152]{2,1,0:T(8,128)(2,1)} fusion(bf16[1,256,1152]{2,1,0:T(8,128)(2,1)S(1)} %get-tuple-element.10, bf16[1,256,1152]{2,1,0:T(8,128)(2,1)S(1)} %get-tuple-element.11, bf16[1,256,1152]{2,1,0:T(8,128)(2,1)S(1)} %get-tuple-element.9), kind=kLoop, calls=%fused_computation.11 | loop fusion | flops 1769472 | bytes 3538944 | tf_op jit(solution)/shard_map/stack | solution.py:85
  34.5 4.0 %collective-permute-start.2 = (bf16[3,256,1152]{2,1,0:T(8,128)(2,1)}, bf16[3,256,1152]{2,1,0:T(8,128)(2,1)}, u32[]{:S(2)}, u32[]{:S(2)}) collective-permute-start(bf16[3,256,1152]{2,1,0:T(8,128)(2,1)} %pad_maximum_fusion), channel_id=1, source_target_pairs={{0,1},{1,0},{2,3},{3,2},{4,5},{5,4},{6,7},{7,6},{8,9},{9,8},{10,11... | collective-permute-start | bytes 5308424 | tf_op jit(solution)/shard_map/ppermute | solution.py:85
  38.5 1.9 %collective-permute-start.3 = (bf16[256,512]{1,0:T(8,128)(2,1)S(1)}, bf16[256,512]{1,0:T(8,128)(2,1)S(1)}, u32[]{:S(2)}, u32[]{:S(2)}) collective-permute-start(bf16[256,512]{1,0:T(8,128)(2,1)S(1)} %copy-done.2), channel_id=1, source_target_pairs={{0,1},{1,0},{2,3},{3,2},{4,5},{5,4},{6,7},{7,6},{8,9},{9,8},{10,11... | collective-permute-start | bytes 786440 | tf_op jit(solution)/shard_map/ppermute | solution.py:86
  40.4 0.4 fusion.11
  40.8 1.3 %collective-permute-done.3 = bf16[256,512]{1,0:T(8,128)(2,1)S(1)} collective-permute-done((bf16[256,512]{1,0:T(8,128)(2,1)S(1)}, bf16[256,512]{1,0:T(8,128)(2,1)S(1)}, u32[]{:S(2)}, u32[]{:S(2)}) %collective-permute-start.3) | collective-permute-done | bytes 262176 | tf_op jit(solution)/shard_map/ppermute | solution.py:86
  42.1 2.3 %fusion.6 = bf16[1152,256]{1,0:T(8,128)(2,1)} fusion(f32[1152,256]{1,0:T(8,128)S(1)} %fusion.11, bf16[3,256,1152]{2,1,0:T(8,128)(2,1)} %collective-permute-done.2, bf16[256,512]{1,0:T(8,128)(2,1)S(1)} %collective-permute-done.3, u32[]{:T(128)S(6)} %mul.84), kind=kOutput, calls=%fused_computation.10 | convolution fusion | flops 151584768 | bytes 2490372 | tf_op jit(solution)/shard_map/dot_general | solution.py:63
  44.4 4.4 %collective-permute-start.5 = (bf16[1152,256]{1,0:T(8,128)(2,1)}, bf16[1152,256]{1,0:T(8,128)(2,1)S(1)}, u32[]{:S(2)}, u32[]{:S(2)}) collective-permute-start(bf16[1152,256]{1,0:T(8,128)(2,1)} %fusion.6), channel_id=1, source_target_pairs={{0,192},{1,577},{192,384},{193,1},{384,576},{385,193},{576,0},{577... | collective-permute-start | bytes 1769480 | tf_op jit(solution)/shard_map/ppermute | solution.py:95
  48.8 0.4 fusion.7
  49.2 0.4 fusion.9
  49.6 1.5 %fusion.5 = bf16[1152,256]{1,0:T(8,128)(2,1)S(1)} fusion(f32[1152,256]{1,0:T(8,128)S(1)} %fusion.9, bf16[3,256,1152]{2,1,0:T(8,128)(2,1)} %collective-permute-done.2, bf16[256,512]{1,0:T(8,128)(2,1)S(1)} %collective-permute-done.3, u32[]{:T(128)S(6)} %mul.89), kind=kOutput, calls=%fused_computation.9 | convolution fusion | flops 151584768 | bytes 2490372 | tf_op jit(solution)/shard_map/dot_general | solution.py:63
  51.1 2.6 %collective-permute-start.4 = (bf16[1152,256]{1,0:T(8,128)(2,1)S(1)}, bf16[1152,256]{1,0:T(8,128)(2,1)S(1)}, u32[]{:S(2)}, u32[]{:S(2)}) collective-permute-start(bf16[1152,256]{1,0:T(8,128)(2,1)S(1)} %fusion.5), channel_id=1, source_target_pairs={{0,193},{1,576},{192,385},{193,0},{384,577},{385,192},{576,1},{577... | collective-permute-start | bytes 1769480 | tf_op jit(solution)/shard_map/ppermute | solution.py:96
  53.7 2.3 %collective-permute-done.5 = bf16[1152,256]{1,0:T(8,128)(2,1)S(1)} collective-permute-done((bf16[1152,256]{1,0:T(8,128)(2,1)}, bf16[1152,256]{1,0:T(8,128)(2,1)S(1)}, u32[]{:S(2)}, u32[]{:S(2)}) %collective-permute-start.5) | collective-permute-done | bytes 589856 | tf_op jit(solution)/shard_map/ppermute | solution.py:95
  55.9 1.4 %fusion.3 = bf16[1152,256]{1,0:T(8,128)(2,1)S(1)} fusion(f32[1152,256]{1,0:T(8,128)S(1)} %fusion.7, bf16[1152,256]{1,0:T(8,128)(2,1)S(1)} %collective-permute-done.5, bf16[3,256,1152]{2,1,0:T(8,128)(2,1)} %collective-permute-done.2, bf16[256,512]{1,0:T(8,128)(2,1)S(1)} %collective-permute-done.3, u32[]{:T(128)S(6)} %mul.84), kind=kOutput, calls=%fused_computation.7 | convolution fusion | flops 152174592 | bytes 3080196 | tf_op jit(solution)/shard_map/dot_general | solution.py:63
  57.4 5.3 %collective-permute-start.6 = (bf16[1152,256]{1,0:T(8,128)(2,1)S(1)}, bf16[1152,256]{1,0:T(8,128)(2,1)S(1)}, u32[]{:S(2)}, u32[]{:S(2)}) collective-permute-start(bf16[1152,256]{1,0:T(8,128)(2,1)S(1)} %fusion.3), channel_id=1, source_target_pairs={{0,192},{1,577},{192,384},{193,1},{384,576},{385,193},{576,0},{577... | collective-permute-start | bytes 1769480 | tf_op jit(solution)/shard_map/ppermute | solution.py:98
  62.7 0.4 fusion.13
  63.1 0.9 collective-permute-done.4
  64.0 5.5 %collective-permute-done.6 = bf16[1152,256]{1,0:T(8,128)(2,1)S(1)} collective-permute-done((bf16[1152,256]{1,0:T(8,128)(2,1)S(1)}, bf16[1152,256]{1,0:T(8,128)(2,1)S(1)}, u32[]{:S(2)}, u32[]{:S(2)}) %collective-permute-start.6) | collective-permute-done | bytes 589856 | tf_op jit(solution)/shard_map/ppermute | solution.py:98
  69.5 2.3 %fusion.4 = bf16[1152,256]{1,0:T(8,128)(2,1)} fusion(f32[1152,256]{1,0:T(8,128)S(1)} %fusion.13, bf16[1152,256]{1,0:T(8,128)(2,1)S(1)} %collective-permute-done.6, bf16[1152,256]{1,0:T(8,128)(2,1)S(1)} %collective-permute-done.4, bf16[3,256,1152]{2,1,0:T(8,128)(2,1)} %collective-permute-done.2, bf16[256,512]{1,0:T(8,128)(2,1)S(1)} %collective-permute-done.3, ...), kind=kOutput, calls=%fused_computation.8 | convolution fusion | flops 152764416 | bytes 3670020 | tf_op jit(solution)/shard_map/dot_general | solution.py:63
  71.8 1.2 reshape.23
  73.1 25.8 %all_to_all.10 = bf16[8,12,12,256]{3,2,1,0:T(8,128)(2,1)S(1)} all-to-all(bf16[8,12,12,256]{3,2,1,0:T(8,128)(2,1)S(1)} %copy.11), channel_id=1, replica_groups=mesh['x'=4,'zh'=4,'zl'=3,'y'=8,'c'=2] {'y'}, dimensions={0} | all-to-all | bytes 1179648 | tf_op jit(solution)/shard_map/all_to_all | solution.py:103
  98.9 0.1 reduce_sum.21
  99.1 19.0 %all_to_all.11 = bf16[24,6,256]{2,1,0:T(8,128)(2,1)S(1)} all-to-all(bf16[24,6,256]{2,1,0:T(8,128)(2,1)S(1)} %reshape.24), channel_id=1, replica_groups=mesh['x'=4,'zh'=4,'zl'=3,'y'=8,'c'=2] {'zh','zl','c'}, dimensions={0} | all-to-all | bytes 147456 | tf_op jit(solution)/shard_map/all_to_all | solution.py:105
  118.2 0.6 multiply_subtract_fusion
  118.8 2.3 %copy-done.1 = bf16[144,128,128]{2,1,0:T(8,128)(2,1)S(1)} copy-done((bf16[144,128,128]{2,1,0:T(8,128)(2,1)S(1)}, bf16[144,128,128]{2,1,0:T(8,128)(2,1)}, u32[]{:S(2)}) %copy-start.1) | copy-done | bytes 4718616
  121.2 3.3 %shard_map.102 = bf16[256,512]{1,0:T(8,128)(2,1)} custom-call(bf16[256,4608]{1,0:T(8,128)(2,1)S(1)} %copy-done, bf16[16,9,128,128]{3,2,1,0:T(8,128)(2,1)S(1)} %bitcast.26), custom_call_target="tpu_custom_call" | custom-call | flops 1207959552 | bytes 7077888 | tf_op jit(solution)/shard_map/pallas_call | solution.py:49
  (23 shorter events, 0.3 us)
Async XLA Ops:
  7.2 111.7 %all-gather.3.cloned.1.call-start = ((), (), s32[]{:S(2)}) async-start(), calls=%async_computation.2 | async-start | bytes 5013504 | tf_op jit(solution)/shard_map/all_gather | solution.py:76
  8.8 17.1 %collective-permute-start = (bf16[3,128,128]{2,1,0:T(8,128)(2,1)S(1)}, bf16[3,128,128]{2,1,0:T(8,128)(2,1)S(1)}, u32[]{:S(2)}, u32[]{:S(2)}) collective-permute-start(bf16[3,128,128]{2,1,0:T(8,128)(2,1)S(1)} %get-tuple-element.8), channel_id=1, source_target_pairs={{0,176},{16,0},{32,16},{48,32},{64,48},{80,64},{96,80},{112,96},{1... | collective-permute-start | bytes 294920 | tf_op jit(solution)/shard_map/ppermute | solution.py:73
  24.0 6.6 %collective-permute-start.1 = (bf16[3,128,128]{2,1,0:T(8,128)(2,1)S(1)}, bf16[3,128,128]{2,1,0:T(8,128)(2,1)S(1)}, u32[]{:S(2)}, u32[]{:S(2)}) collective-permute-start(bf16[3,128,128]{2,1,0:T(8,128)(2,1)S(1)} %get-tuple-element.8), channel_id=1, source_target_pairs={{0,16},{16,32},{32,48},{48,64},{64,80},{80,96},{96,112},{112,128},... | collective-permute-start | bytes 294920 | tf_op jit(solution)/shard_map/ppermute | solution.py:72
  33.0 5.5 %copy-start.2 = (bf16[256,512]{1,0:T(8,128)(2,1)S(1)}, bf16[256,512]{1,0:T(8,128)(2,1)}, u32[]{:S(2)}) copy-start(bf16[256,512]{1,0:T(8,128)(2,1)} %param.8) | copy-start | bytes 786436
  33.0 7.4 %copy-start = (bf16[256,4608]{1,0:T(8,128)(2,1)S(1)}, bf16[256,4608]{1,0:T(8,128)(2,1)}, u32[]{:S(2)}) copy-start(bf16[256,4608]{1,0:T(8,128)(2,1)} %tokens_ref.1) | copy-start | bytes 7077892
  34.5 7.7 %collective-permute-start.2 = (bf16[3,256,1152]{2,1,0:T(8,128)(2,1)}, bf16[3,256,1152]{2,1,0:T(8,128)(2,1)}, u32[]{:S(2)}, u32[]{:S(2)}) collective-permute-start(bf16[3,256,1152]{2,1,0:T(8,128)(2,1)} %pad_maximum_fusion), channel_id=1, source_target_pairs={{0,1},{1,0},{2,3},{3,2},{4,5},{5,4},{6,7},{7,6},{8,9},{9,8},{10,11... | collective-permute-start | bytes 5308424 | tf_op jit(solution)/shard_map/ppermute | solution.py:85
  38.5 3.7 %collective-permute-start.3 = (bf16[256,512]{1,0:T(8,128)(2,1)S(1)}, bf16[256,512]{1,0:T(8,128)(2,1)S(1)}, u32[]{:S(2)}, u32[]{:S(2)}) collective-permute-start(bf16[256,512]{1,0:T(8,128)(2,1)S(1)} %copy-done.2), channel_id=1, source_target_pairs={{0,1},{1,0},{2,3},{3,2},{4,5},{5,4},{6,7},{7,6},{8,9},{9,8},{10,11... | collective-permute-start | bytes 786440 | tf_op jit(solution)/shard_map/ppermute | solution.py:86
  44.4 11.5 %collective-permute-start.5 = (bf16[1152,256]{1,0:T(8,128)(2,1)}, bf16[1152,256]{1,0:T(8,128)(2,1)S(1)}, u32[]{:S(2)}, u32[]{:S(2)}) collective-permute-start(bf16[1152,256]{1,0:T(8,128)(2,1)} %fusion.6), channel_id=1, source_target_pairs={{0,192},{1,577},{192,384},{193,1},{384,576},{385,193},{576,0},{577... | collective-permute-start | bytes 1769480 | tf_op jit(solution)/shard_map/ppermute | solution.py:95
  51.1 12.9 %collective-permute-start.4 = (bf16[1152,256]{1,0:T(8,128)(2,1)S(1)}, bf16[1152,256]{1,0:T(8,128)(2,1)S(1)}, u32[]{:S(2)}, u32[]{:S(2)}) collective-permute-start(bf16[1152,256]{1,0:T(8,128)(2,1)S(1)} %fusion.5), channel_id=1, source_target_pairs={{0,193},{1,576},{192,385},{193,0},{384,577},{385,192},{576,1},{577... | collective-permute-start | bytes 1769480 | tf_op jit(solution)/shard_map/ppermute | solution.py:96
  57.4 12.1 %collective-permute-start.6 = (bf16[1152,256]{1,0:T(8,128)(2,1)S(1)}, bf16[1152,256]{1,0:T(8,128)(2,1)S(1)}, u32[]{:S(2)}, u32[]{:S(2)}) collective-permute-start(bf16[1152,256]{1,0:T(8,128)(2,1)S(1)} %fusion.3), channel_id=1, source_target_pairs={{0,192},{1,577},{192,384},{193,1},{384,576},{385,193},{576,0},{577... | collective-permute-start | bytes 1769480 | tf_op jit(solution)/shard_map/ppermute | solution.py:98
  73.1 45.1 %copy-start.3 = (f32[6,512]{1,0:T(8,128)S(1)}, f32[6,512]{1,0:T(8,128)}, u32[]{:S(2)}) copy-start(f32[6,512]{1,0:T(8,128)} %param.11) | copy-start | bytes 36868
  73.1 45.1 %copy-start.4 = (f32[6,512]{1,0:T(8,128)S(1)}, f32[6,512]{1,0:T(8,128)}, u32[]{:S(2)}) copy-start(f32[6,512]{1,0:T(8,128)} %param.13) | copy-start | bytes 36868
  73.1 45.1 %copy-start.5 = (f32[6,512]{1,0:T(8,128)S(1)}, f32[6,512]{1,0:T(8,128)}, u32[]{:S(2)}) copy-start(f32[6,512]{1,0:T(8,128)} %param.12) | copy-start | bytes 36868
  118.8 2.3 %copy-start.1 = (bf16[144,128,128]{2,1,0:T(8,128)(2,1)S(1)}, bf16[144,128,128]{2,1,0:T(8,128)(2,1)}, u32[]{:S(2)}) copy-start(bf16[144,128,128]{2,1,0:T(8,128)(2,1)} %all-gather.3.cloned.1.call-done) | copy-start | bytes 14155780
Sparse Core Ops, SparseCore 0:
  31.5 44.5 all-gather.2

commit v2 on v1

v2 whole, which is shorter than its diff:
```python
import jax
import jax.numpy as jnp
from jax import lax
from jax.experimental import pallas as pl
from jax.experimental.pallas import tpu as pltpu
from jax.sharding import Mesh, PartitionSpec as P

BETA_ONE = 0.9
BETA_TWO = 0.99
STEP_SIZE = 0.5
EPSILON = 1e-08
CORRECT_ONE = 1.0 - 0.9**20
CORRECT_TWO = 1.0 - 0.99**20
NX, NZH, NZL, NY, NC = 4, 4, 3, 8, 2
AXES = ("x", "zh", "zl", "y", "c")
BF = jnp.bfloat16
F32 = jnp.float32
SLABS = 6


def project_kernel(tokens_hbm, tiles_ref, out_ref, tokens_ref, weights, sems, tokens_sem):
    blk = tiles_ref.shape[-1]
    cbs = out_ref.shape[1] // blk
    rows = weights.shape[0] // SLABS
    per_slab = (rows // blk) * cbs

    def slab(s):
        return weights.at[pl.ds(s * rows, rows)]

    whole = pltpu.make_async_copy(tokens_hbm, tokens_ref, tokens_sem)
    whole.start()
    for s in range(SLABS):
        for t in range(s * per_slab, (s + 1) * per_slab):
            owner, i = divmod(t, 3)
            z, q = divmod(owner, NY * NC)
            pltpu.make_async_copy(
                tiles_ref.at[q, z * 3 + i],
                weights.at[pl.ds(t // cbs * blk, blk), pl.ds(t % cbs * blk, blk)],
                sems.at[s],
            ).start()
    whole.wait()
    total = None
    for s in range(SLABS):
        pltpu.make_async_copy(slab(s), slab(s), sems.at[s]).wait()
        part = jnp.dot(tokens_ref[:, s * rows : (s + 1) * rows], slab(s)[...], preferred_element_type=F32)
        total = part if total is None else total + part
    out_ref[...] = total.astype(out_ref.dtype)


def project(tokens, tiles, columns):
    rows, width = tokens.shape
    return pl.pallas_call(
        project_kernel,
        out_shape=jax.ShapeDtypeStruct((rows, columns), BF),
        in_specs=[pl.BlockSpec(memory_space=pl.ANY), pl.BlockSpec(memory_space=pl.ANY)],
        out_specs=pl.BlockSpec(memory_space=pltpu.VMEM),
        scratch_shapes=[
            pltpu.VMEM((rows, width), BF),
            pltpu.VMEM((width, columns), BF),
            pltpu.SemaphoreType.DMA((SLABS,)),
            pltpu.SemaphoreType.DMA,
        ],
        compiler_params=pltpu.CompilerParams(vmem_limit_bytes=60 * 2**20),
        cost_estimate=pl.CostEstimate(
            flops=2 * rows * width * columns, bytes_accessed=2 * (rows * width + width * columns), transcendentals=0
        ),
    )(tokens, tiles)


def thirds_kernel(zl_ref, own, above, below, after, out):
    size = own.shape[0]
    for k, third in enumerate((own, above, below)):
        at = zl_ref[0] + k
        at = jnp.where(at >= NZL, at - NZL, at)
        out[pl.ds(at * size, size)] = third[...]


def in_z_order(zl, own, above, below, after):
    vmem = pl.BlockSpec(memory_space=pltpu.VMEM)
    return pl.pallas_call(
        thirds_kernel,
        out_shape=jax.ShapeDtypeStruct((NZL * own.shape[0], *own.shape[1:]), BF),
        in_specs=[pl.BlockSpec(memory_space=pltpu.SMEM), vmem, vmem, vmem, pl.BlockSpec(memory_space=pl.ANY)],
        out_specs=vmem,
        cost_estimate=pl.CostEstimate(flops=0, bytes_accessed=4 * NZL * own.size, transcendentals=0),
    )(zl, own, above, below, after)


def adam_kernel(terms, master, first, second, after, new_first, new_second, new_weight):
    half = terms.shape[-1]
    total = jnp.sum(terms[...].astype(F32), axis=0)
    for k in range(NC):
        at = slice(k * half, (k + 1) * half)
        gradient = total[k]
        one = BETA_ONE * first[:, at] + (1.0 - BETA_ONE) * gradient
        two = BETA_TWO * second[:, at] + (1.0 - BETA_TWO) * gradient * gradient
        new_first[:, at] = one
        new_second[:, at] = two
        new_weight[:, at] = master[:, at] - STEP_SIZE * (
            one / CORRECT_ONE / (jnp.sqrt(two / CORRECT_TWO) + EPSILON)
        )


def adam(terms, master, first, second, after):
    vmem = pl.BlockSpec(memory_space=pltpu.VMEM)
    shape = jax.ShapeDtypeStruct(master.shape, F32)
    return pl.pallas_call(
        adam_kernel,
        out_shape=(shape, shape, shape),
        in_specs=[vmem] * 4 + [pl.BlockSpec(memory_space=pl.ANY)],
        out_specs=(vmem, vmem, vmem),
        cost_estimate=pl.CostEstimate(flops=20 * master.size, bytes_accessed=24 * master.size + 2 * terms.size, transcendentals=0),
    )(terms, master, first, second, after)


def dot_t(a, b):
    return lax.dot_general(a, b, (((0,), (0,)), ((), ())), preferred_element_type=F32)


def local(tokens, cot, codes, scales, master, first, second):
    width, columns = tokens.shape[1], cot.shape[1]
    x, zl, c = (lax.axis_index(a).astype(jnp.uint32) for a in ("x", "zl", "c"))
    nz = NZH * NZL
    swap = [(0, 1), (1, 0)]
    z_up = [(i, (i + 1) % nz) for i in range(nz)]
    z_down = [(i, (i - 1) % nz) for i in range(nz)]

    theirs = lax.ppermute(tokens, "c", swap)
    cot_theirs = lax.ppermute(cot, "c", swap)

    w = (codes.astype(F32) * scales.astype(F32)).astype(BF)
    below = lax.ppermute(w, ("zh", "zl"), z_up)
    above = lax.ppermute(w, ("zh", "zl"), z_down)

    chunk, half = width // NX, columns // 2
    on = x + 1 + 2 * c

    def part(k, j):
        return lax.dynamic_slice_in_dim(k, (j & (NX - 1)) * chunk, chunk, axis=1)

    near = [lax.dynamic_slice_in_dim(k, c * half, half, axis=1) for k in (cot, cot_theirs)]
    far = [lax.dynamic_slice_in_dim(k, (1 - c) * half, half, axis=1) for k in (cot, cot_theirs)]

    def term(j, cots):
        return dot_t(part(tokens, j), cots[0]) + dot_t(part(theirs, j), cots[1])

    straight = [(2 * i + d, 2 * ((i + 1 - 2 * d) % NX) + d) for i in range(NX) for d in range(2)]
    crossed = [(2 * i + d, 2 * ((i + 1 - 2 * d) % NX) + 1 - d) for i in range(NX) for d in range(2)]
    two_on = term(x + 2, near).astype(BF)
    tiles = in_z_order(zl.astype(jnp.int32).reshape(1), w, above, below, two_on)
    tiles = lax.all_gather(tiles, ("y", "c"), axis=0)
    two_on = lax.ppermute(two_on, ("x", "c"), straight)
    one_far = lax.ppermute(term(on, far).astype(BF), ("x", "c"), crossed)
    one_near = (term(on, near) + two_on.astype(F32)).astype(BF)
    one_near = lax.ppermute(one_near, ("x", "c"), straight)
    summed = (term(x, near) + one_far.astype(F32) + one_near.astype(F32)).astype(BF)

    rows = chunk // (nz * NY)
    thirds = summed.reshape(NZH, NZL, NY * rows, half)

    def third(j):
        return lax.dynamic_index_in_dim(thirds, jnp.where(j > 2, j - 3, j), axis=1, keepdims=False)

    up = lax.ppermute(third(zl + 1), ("zh", "zl"), z_up)
    down = lax.ppermute(third(zl + 2), ("zh", "zl"), z_down)
    by_z = (third(zl).astype(F32) + up.astype(F32) + down.astype(F32)).astype(BF)
    last = by_z.reshape(NZH * NY * NC, rows // NC, half)
    last = lax.all_to_all(last, ("zh", "y", "c"), 0, 0, tiled=True)
    last = last.reshape(NZH * NY, NC, rows // NC, half)

    projected = project(tokens, tiles, columns)
    return projected, *adam(last, master, first, second, projected)


def solution(mesh):
    fine = Mesh(mesh.devices.reshape(NX, NZH, NZL, NY, NC), AXES)
    rows = P(AXES, None)
    tiles = P(("zl", "y", "c"), None, None)
    return jax.shard_map(
        local,
        mesh=fine,
        in_specs=(rows, rows, tiles, tiles, rows, rows, rows),
        out_specs=(rows, rows, rows, rows),
        check_vma=False,
    )
```

time: 132 us -> 120 us (0.909)
  blocking collectives: 44.8 us -> 0 us
  starting transfers between devices: 35.3 us -> 57.3 us
  waiting for transfers between devices: 14.6 us -> 23.9 us
  Pallas kernels: 3.33 us -> 9.04 us
  local copies, waits for them, and re-layouts: 6.06 us -> 1.52 us
  matrix products: 9.02 us -> 11.5 us
  other arithmetic: 3.86 us -> 2.31 us
    all_to_all x2 -> x0, blocking collectives: 44.8 us -> none  [the longest x1 25.8 us: local(): by_y = lax.all_to_all(by_y, 'y', 0, 0, tiled=True)]
    all_to_all x0 -> x1, starting transfers between devices: none -> 16.1 us  [local(): last = lax.all_to_all(last, ('zh', 'y', 'c'), 0, 0, tiled=True)]
    all_to_all x0 -> x1, waiting for transfers between devices: none -> 13.5 us  [local(): last = lax.all_to_all(last, ('zh', 'y', 'c'), 0, 0, tiled=True)]
    ppermute x5 -> x7, starting transfers between devices: 28 us -> 34.7 us  [the longest x1 12.4 us: local(): theirs = lax.ppermute(tokens, 'c', swap)]
    pallas_call x0 -> x2, Pallas kernels: none -> 3.38 us  [the longest x1 1.71 us: in_z_order(): pl.pallas_call(thirds_kernel, out_shape=jax.ShapeDtypeStruct((NZL * own.s...]
    ppermute x5 -> x7, waiting for transfers between devices: 7.79 us -> 5.11 us  [the longest x1 1.51 us: local(): up = lax.ppermute(third(zl + 1), ('zh', 'zl'), z_up)]
    dot_general x8, matrix products: 9.02 us -> 11.5 us  [dot_t(): lax.dot_general(a, b, (((0,), (0,)), ((), ())), preferred_element_type=F32)]
    pallas_call x1, Pallas kernels: 3.33 us -> 5.66 us  [project(): pl.pallas_call(project_kernel, out_shape=jax.ShapeDtypeStruct((rows, colu...]
  transfers between devices with their start and end apart: 8 -> 11, of which waited for: 5 -> 6; matrix products, arithmetic and copies ran while one was open for 11% -> 12% of each run, Pallas kernels for 0% -> 5%
where the time goes in v2:
time: 120 us
  starting transfers between devices  57.3 us (48%)
  waiting for transfers between devices  23.9 us (20%)
  between operations  14.3 us (12%)
  matrix products  11.5 us (10%)
  Pallas kernels  9.04 us (8%)
  other arithmetic  2.31 us (2%)
  local copies, waits for them, and re-layouts  1.52 us (1%)
    all_to_all x1, starting transfers between devices, local(): last = lax.all_to_all(last, ('zh', 'y', 'c'), 0, 0, tiled=True)  16.1 us
    all_to_all x1, waiting for transfers between devices, local(): last = lax.all_to_all(last, ('zh', 'y', 'c'), 0, 0, tiled=True)  13.5 us
    ppermute x1, starting transfers between devices, local(): theirs = lax.ppermute(tokens, 'c', swap)  12.4 us
    dot_general x8, matrix products, dot_t(): lax.dot_general(a, b, (((0,), (0,)), ((), ())), preferred_element_type=F32)  11.5 us
    pallas_call x1, Pallas kernels, project(): pl.pallas_call(project_kernel, out_shape=jax.ShapeDtypeStruct((rows, colu...  5.66 us
    ppermute x1, starting transfers between devices, local(): above = lax.ppermute(w, ('zh', 'zl'), z_down)  5.28 us
    ppermute x1, waiting for transfers between devices, local(): one_near = lax.ppermute(one_near, ('x', 'c'), straight)  5.26 us
    ppermute x1, starting transfers between devices, local(): one_near = lax.ppermute(one_near, ('x', 'c'), straight)  4.61 us
  transfers between devices with their start and end apart: 11, of which 6 were waited for; matrix products, arithmetic and copies ran while one was open for 12% of the time, Pallas kernels for 5%

profile of v2, /device:TPU:1, one launch (start us, length us, event | category | flops | bytes accessed | tf_op | source)
XLA Modules:
  0.0 119.8 jit_solution(14408212382494270760)
XLA Ops:
  7.2 12.4 %collective-permute-start.2 = (bf16[256,4608]{1,0:T(8,128)(2,1)}, bf16[256,4608]{1,0:T(8,128)(2,1)}, u32[]{:S(2)}, u32[]{:S(2)}) collective-permute-start(bf16[256,4608]{1,0:T(8,128)(2,1)} %tokens_hbm.1), channel_id=1, source_target_pairs={{0,1},{1,0},{2,3},{3,2},{4,5},{5,4},{6,7},{7,6},{8,9},{9,8},{10,11... | collective-permute-start | bytes 7077896 | tf_op jit(solution)/shard_map/ppermute | solution.py:128
  19.6 1.9 %collective-permute-start.3 = (bf16[256,512]{1,0:T(8,128)(2,1)}, bf16[256,512]{1,0:T(8,128)(2,1)S(1)}, u32[]{:S(2)}, u32[]{:S(2)}) collective-permute-start(bf16[256,512]{1,0:T(8,128)(2,1)} %param.8), channel_id=1, source_target_pairs={{0,1},{1,0},{2,3},{3,2},{4,5},{5,4},{6,7},{7,6},{8,9},{9,8},{10,11... | collective-permute-start | bytes 786440 | tf_op jit(solution)/shard_map/ppermute | solution.py:129
  21.6 0.7 bitcast_convert_fusion
  22.3 1.6 %multiply_convert_fusion.own = bf16[3,128,128]{2,1,0:T(8,128)(2,1)} fusion(bf16[3,128,128]{2,1,0:T(8,128)(2,1)} %param.9, f32[3,128]{1,0:T(4,128)S(1)} %bitcast_convert_fusion), kind=kLoop, calls=%fused_computation.28 | loop fusion | flops 147456 | bytes 198144 | tf_op jit(solution)/shard_map/convert_element_type | solution.py:131
  23.8 5.3 %collective-permute-start = (bf16[3,128,128]{2,1,0:T(8,128)(2,1)}, bf16[3,128,128]{2,1,0:T(8,128)(2,1)}, u32[]{:S(2)}, u32[]{:S(2)}) collective-permute-start(bf16[3,128,128]{2,1,0:T(8,128)(2,1)} %multiply_convert_fusion.own), channel_id=1, source_target_pairs={{0,176},{16,0},{32,16},{48,32},{64,48},{80,64},{96,80},{112,96},{1... | collective-permute-start | bytes 294920 | tf_op jit(solution)/shard_map/ppermute | solution.py:133
  29.1 1.9 %collective-permute-start.1 = (bf16[3,128,128]{2,1,0:T(8,128)(2,1)}, bf16[3,128,128]{2,1,0:T(8,128)(2,1)}, u32[]{:S(2)}, u32[]{:S(2)}) collective-permute-start(bf16[3,128,128]{2,1,0:T(8,128)(2,1)} %multiply_convert_fusion.own), channel_id=1, source_target_pairs={{0,16},{16,32},{32,48},{48,64},{64,80},{80,96},{96,112},{112,128},... | collective-permute-start | bytes 294920 | tf_op jit(solution)/shard_map/ppermute | solution.py:132
  31.1 1.5 %fusion.11 = f32[1152,256]{1,0:T(8,128)S(1)} fusion(bf16[256,4608]{1,0:T(8,128)(2,1)} %tokens_hbm.1, u32[]{:T(128)S(6)} %mul.42, bf16[256,512]{1,0:T(8,128)(2,1)} %param.8, u32[]{:T(128)S(6)} %mul.43), kind=kOutput, calls=%fused_computation.15 | convolution fusion | flops 150994944 | bytes 1900552 | tf_op jit(solution)/shard_map/dot_general | solution.py:117
  32.5 2.4 %fusion.5.after = bf16[1152,256]{1,0:T(8,128)(2,1)} fusion(f32[1152,256]{1,0:T(8,128)S(1)} %fusion.11, bf16[256,4608]{1,0:T(8,128)(2,1)} %collective-permute-done.2, u32[]{:T(128)S(6)} %mul.42, bf16[256,512]{1,0:T(8,128)(2,1)S(1)} %collective-permute-done.3, u32[]{:T(128)S(6)} %mul.43), kind=kOutput, calls=%fused_computation.9 | convolution fusion | flops 151584768 | bytes 2490376 | tf_op jit(solution)/shard_map/dot_general | solution.py:117
  35.0 1.0 collective-permute-done.1.below
  36.0 1.7 %shard_map.102 = bf16[9,128,128]{2,1,0:T(8,128)(2,1)} custom-call(s32[1]{0:T(128)} %bitcast.zl_ref, bf16[3,128,128]{2,1,0:T(8,128)(2,1)} %multiply_convert_fusion.own, bf16[3,128,128]{2,1,0:T(8,128)(2,1)} %collective-permute-done.above, bf16[3,128,128]{2,1,0:T(8,128)(2,1)} %collective-permute-done.1.below, bf16[1152,256]{1,0:T(8,128)(2,1)} %fusion.5.after), custom_call_target="tpu_custom_call" | custom-call | bytes 589824 | tf_op jit(solution)/shard_map/pallas_call | solution.py:80
  37.7 4.4 %collective-permute-start.5 = (bf16[1152,256]{1,0:T(8,128)(2,1)S(1)}, bf16[1152,256]{1,0:T(8,128)(2,1)}, u32[]{:S(2)}, u32[]{:S(2)}) collective-permute-start(bf16[1152,256]{1,0:T(8,128)(2,1)S(1)} %copy-done.1), channel_id=1, source_target_pairs={{0,192},{1,577},{192,384},{193,1},{384,576},{385,193},{576,0},{577... | collective-permute-start | bytes 1769480 | tf_op jit(solution)/shard_map/ppermute | solution.py:152
  42.2 0.4 fusion.15
  42.6 0.4 fusion.17
  42.9 2.3 %fusion.6 = bf16[1152,256]{1,0:T(8,128)(2,1)} fusion(f32[1152,256]{1,0:T(8,128)S(1)} %fusion.17, bf16[256,4608]{1,0:T(8,128)(2,1)} %collective-permute-done.2, u32[]{:T(128)S(6)} %mul.46, bf16[256,512]{1,0:T(8,128)(2,1)S(1)} %collective-permute-done.3, u32[]{:T(128)S(6)} %mul.47), kind=kOutput, calls=%fused_computation.10 | convolution fusion | flops 151584768 | bytes 2490376 | tf_op jit(solution)/shard_map/dot_general | solution.py:117
  45.2 4.2 %collective-permute-start.4 = (bf16[1152,256]{1,0:T(8,128)(2,1)}, bf16[1152,256]{1,0:T(8,128)(2,1)}, u32[]{:S(2)}, u32[]{:S(2)}) collective-permute-start(bf16[1152,256]{1,0:T(8,128)(2,1)} %fusion.6), channel_id=1, source_target_pairs={{0,193},{1,576},{192,385},{193,0},{384,577},{385,192},{576,1},{577... | collective-permute-start | bytes 1769480 | tf_op jit(solution)/shard_map/ppermute | solution.py:153
  49.4 2.5 %fusion.3 = bf16[1152,256]{1,0:T(8,128)(2,1)} fusion(f32[1152,256]{1,0:T(8,128)S(1)} %fusion.15, bf16[1152,256]{1,0:T(8,128)(2,1)} %collective-permute-done.5, bf16[256,4608]{1,0:T(8,128)(2,1)} %collective-permute-done.2, u32[]{:T(128)S(6)} %mul.46, bf16[256,512]{1,0:T(8,128)(2,1)S(1)} %collective-permute-done.3, u32[]{:T(128)S(6)} %mul.43), kind=kOutput, calls=%fused_computation.7 | convolution fusion | flops 152174592 | bytes 3080200 | tf_op jit(solution)/shard_map/dot_general | solution.py:117
  51.9 4.6 %collective-permute-start.6 = (bf16[1152,256]{1,0:T(8,128)(2,1)}, bf16[1152,256]{1,0:T(8,128)(2,1)S(1)}, u32[]{:S(2)}, u32[]{:S(2)}) collective-permute-start(bf16[1152,256]{1,0:T(8,128)(2,1)} %fusion.3), channel_id=1, source_target_pairs={{0,192},{1,577},{192,384},{193,1},{384,576},{385,193},{576,0},{577... | collective-permute-start | bytes 1769480 | tf_op jit(solution)/shard_map/ppermute | solution.py:155
  56.5 0.4 fusion.8
  56.9 1.5 %collective-permute-done.4 = bf16[1152,256]{1,0:T(8,128)(2,1)} collective-permute-done((bf16[1152,256]{1,0:T(8,128)(2,1)}, bf16[1152,256]{1,0:T(8,128)(2,1)}, u32[]{:S(2)}, u32[]{:S(2)}) %collective-permute-start.4) | collective-permute-done | bytes 589856 | tf_op jit(solution)/shard_map/ppermute | solution.py:153
  58.4 5.3 %collective-permute-done.6 = bf16[1152,256]{1,0:T(8,128)(2,1)S(1)} collective-permute-done((bf16[1152,256]{1,0:T(8,128)(2,1)}, bf16[1152,256]{1,0:T(8,128)(2,1)S(1)}, u32[]{:S(2)}, u32[]{:S(2)}) %collective-permute-start.6) | collective-permute-done | bytes 589856 | tf_op jit(solution)/shard_map/ppermute | solution.py:155
  63.6 1.7 %fusion.4 = bf16[1152,256]{1,0:T(8,128)(2,1)S(1)} fusion(f32[1152,256]{1,0:T(8,128)S(1)} %fusion.8, bf16[1152,256]{1,0:T(8,128)(2,1)S(1)} %collective-permute-done.6, bf16[1152,256]{1,0:T(8,128)(2,1)} %collective-permute-done.4, bf16[256,4608]{1,0:T(8,128)(2,1)} %collective-permute-done.2, u32[]{:T(128)S(6)} %mul.44, ...), kind=kOutput, calls=%fused_computation.8 | convolution fusion | flops 152764416 | bytes 3670024 | tf_op jit(solution)/shard_map/dot_general | solution.py:117
  65.4 1.9 %collective-permute-start.7 = (bf16[4,96,256]{2,1,0:T(8,128)(2,1)S(1)}, bf16[4,96,256]{2,1,0:T(8,128)(2,1)S(1)}, u32[]{:S(2)}, u32[]{:S(2)}) collective-permute-start(bf16[4,96,256]{2,1,0:T(8,128)(2,1)S(1)} %get-tuple-element.10), channel_id=1, source_target_pairs={{0,16},{16,32},{32,48},{48,64},{64,80},{80,96},{96,112},{112,128},... | collective-permute-start | bytes 589832 | tf_op jit(solution)/shard_map/ppermute | solution.py:164
  67.3 4.6 %collective-permute-start.8 = (bf16[4,96,256]{2,1,0:T(8,128)(2,1)S(1)}, bf16[4,96,256]{2,1,0:T(8,128)(2,1)S(1)}, u32[]{:S(2)}, u32[]{:S(2)}) collective-permute-start(bf16[4,96,256]{2,1,0:T(8,128)(2,1)S(1)} %get-tuple-element.11), channel_id=1, source_target_pairs={{0,176},{16,0},{32,16},{48,32},{64,48},{80,64},{96,80},{112,96},{1... | collective-permute-start | bytes 589832 | tf_op jit(solution)/shard_map/ppermute | solution.py:165
  71.9 1.5 %collective-permute-done.7 = bf16[4,96,256]{2,1,0:T(8,128)(2,1)S(1)} collective-permute-done((bf16[4,96,256]{2,1,0:T(8,128)(2,1)S(1)}, bf16[4,96,256]{2,1,0:T(8,128)(2,1)S(1)}, u32[]{:S(2)}, u32[]{:S(2)}) %collective-permute-start.7) | collective-permute-done | bytes 196640 | tf_op jit(solution)/shard_map/ppermute | solution.py:164
  73.4 1.1 collective-permute-done.8
  74.5 0.1 fusion.20
  74.6 0.8 reshape.24
  75.4 16.1 %all-to-all-start = ((bf16[64,6,256]{2,1,0:T(8,128)(2,1)}), bf16[64,6,256]{2,1,0:T(8,128)(2,1)S(1)}, u32[]{:S(2)}, u32[]{:S(2)}) async-start(bf16[64,6,256]{2,1,0:T(8,128)(2,1)} %reshape.24), calls=%async_computation | async-start | bytes 524288 | tf_op jit(solution)/shard_map/all_to_all | solution.py:168
  91.5 5.7 %shard_map.103.after = bf16[256,512]{1,0:T(8,128)(2,1)} custom-call(bf16[256,4608]{1,0:T(8,128)(2,1)} %tokens_hbm.1, bf16[16,9,128,128]{3,2,1,0:T(8,128)(2,1)} %bitcast.16), custom_call_target="tpu_custom_call" | custom-call | flops 1207959552 | bytes 7077888 | tf_op jit(solution)/shard_map/pallas_call | solution.py:52
  97.1 13.5 %all-to-all-done = bf16[64,6,256]{2,1,0:T(8,128)(2,1)S(1)} async-done(((bf16[64,6,256]{2,1,0:T(8,128)(2,1)}), bf16[64,6,256]{2,1,0:T(8,128)(2,1)S(1)}, u32[]{:S(2)}, u32[]{:S(2)}) %all-to-all-start) | async-done | bytes 196640 | tf_op jit(solution)/shard_map/all_to_all | solution.py:168
  110.6 0.7 copy-done.3
  111.3 1.7 %shard_map.104 = (f32[6,512]{1,0:T(8,128)}, f32[6,512]{1,0:T(8,128)}, f32[6,512]{1,0:T(8,128)}) custom-call(bf16[32,2,6,256]{3,2,1,0:T(8,128)(2,1)} %bitcast.19, f32[6,512]{1,0:T(8,128)} %master.1, f32[6,512]{1,0:T(8,128)} %first.1, f32[6,512]{1,0:T(8,128)} %second.1, bf16[256,512]{1,0:T(8,128)(2,1)} %shard_map.103.after), custom_call_target="tpu_custom_call" | custom-call | flops 61440 | bytes 270336 | tf_op jit(solution)/shard_map/pallas_call | solution.py:107
  (15 shorter events, 0.1 us)
Async XLA Ops:
  7.2 84.3 %all-gather.3.cloned.1.call-start = ((), (), s32[]{:S(2)}) async-start(), calls=%async_computation.1 | async-start | bytes 5013504 | tf_op jit(solution)/shard_map/all_gather | solution.py:151
  7.2 25.3 %collective-permute-start.2 = (bf16[256,4608]{1,0:T(8,128)(2,1)}, bf16[256,4608]{1,0:T(8,128)(2,1)}, u32[]{:S(2)}, u32[]{:S(2)}) collective-permute-start(bf16[256,4608]{1,0:T(8,128)(2,1)} %tokens_hbm.1), channel_id=1, source_target_pairs={{0,1},{1,0},{2,3},{3,2},{4,5},{5,4},{6,7},{7,6},{8,9},{9,8},{10,11... | collective-permute-start | bytes 7077896 | tf_op jit(solution)/shard_map/ppermute | solution.py:128
  19.6 12.9 %collective-permute-start.3 = (bf16[256,512]{1,0:T(8,128)(2,1)}, bf16[256,512]{1,0:T(8,128)(2,1)S(1)}, u32[]{:S(2)}, u32[]{:S(2)}) collective-permute-start(bf16[256,512]{1,0:T(8,128)(2,1)} %param.8), channel_id=1, source_target_pairs={{0,1},{1,0},{2,3},{3,2},{4,5},{5,4},{6,7},{7,6},{8,9},{9,8},{10,11... | collective-permute-start | bytes 786440 | tf_op jit(solution)/shard_map/ppermute | solution.py:129
  23.8 11.1 %collective-permute-start = (bf16[3,128,128]{2,1,0:T(8,128)(2,1)}, bf16[3,128,128]{2,1,0:T(8,128)(2,1)}, u32[]{:S(2)}, u32[]{:S(2)}) collective-permute-start(bf16[3,128,128]{2,1,0:T(8,128)(2,1)} %multiply_convert_fusion.own), channel_id=1, source_target_pairs={{0,176},{16,0},{32,16},{48,32},{64,48},{80,64},{96,80},{112,96},{1... | collective-permute-start | bytes 294920 | tf_op jit(solution)/shard_map/ppermute | solution.py:133
  29.1 6.9 %collective-permute-start.1 = (bf16[3,128,128]{2,1,0:T(8,128)(2,1)}, bf16[3,128,128]{2,1,0:T(8,128)(2,1)}, u32[]{:S(2)}, u32[]{:S(2)}) collective-permute-start(bf16[3,128,128]{2,1,0:T(8,128)(2,1)} %multiply_convert_fusion.own), channel_id=1, source_target_pairs={{0,16},{16,32},{32,48},{48,64},{64,80},{80,96},{96,112},{112,128},... | collective-permute-start | bytes 294920 | tf_op jit(solution)/shard_map/ppermute | solution.py:132
  32.5 9.6 %copy-start = (bf16[256,4608]{1,0:T(8,128)(2,1)S(1)}, bf16[256,4608]{1,0:T(8,128)(2,1)}, u32[]{:S(2)}) copy-start(bf16[256,4608]{1,0:T(8,128)(2,1)} %tokens_hbm.1) | copy-start | bytes 7077892
  34.9 2.8 %copy-start.1 = (bf16[1152,256]{1,0:T(8,128)(2,1)S(1)}, bf16[1152,256]{1,0:T(8,128)(2,1)}, u32[]{:S(2)}) copy-start(bf16[1152,256]{1,0:T(8,128)(2,1)} %fusion.5.after) | copy-start | bytes 1769476
  34.9 7.2 %copy-start.2 = (bf16[256,512]{1,0:T(8,128)(2,1)S(1)}, bf16[256,512]{1,0:T(8,128)(2,1)}, u32[]{:S(2)}) copy-start(bf16[256,512]{1,0:T(8,128)(2,1)} %param.8) | copy-start | bytes 786436
  37.7 11.7 %collective-permute-start.5 = (bf16[1152,256]{1,0:T(8,128)(2,1)S(1)}, bf16[1152,256]{1,0:T(8,128)(2,1)}, u32[]{:S(2)}, u32[]{:S(2)}) collective-permute-start(bf16[1152,256]{1,0:T(8,128)(2,1)S(1)} %copy-done.1), channel_id=1, source_target_pairs={{0,192},{1,577},{192,384},{193,1},{384,576},{385,193},{576,0},{577... | collective-permute-start | bytes 1769480 | tf_op jit(solution)/shard_map/ppermute | solution.py:152
  45.2 13.2 %collective-permute-start.4 = (bf16[1152,256]{1,0:T(8,128)(2,1)}, bf16[1152,256]{1,0:T(8,128)(2,1)}, u32[]{:S(2)}, u32[]{:S(2)}) collective-permute-start(bf16[1152,256]{1,0:T(8,128)(2,1)} %fusion.6), channel_id=1, source_target_pairs={{0,193},{1,576},{192,385},{193,0},{384,577},{385,192},{576,1},{577... | collective-permute-start | bytes 1769480 | tf_op jit(solution)/shard_map/ppermute | solution.py:153
  51.9 11.7 %collective-permute-start.6 = (bf16[1152,256]{1,0:T(8,128)(2,1)}, bf16[1152,256]{1,0:T(8,128)(2,1)S(1)}, u32[]{:S(2)}, u32[]{:S(2)}) collective-permute-start(bf16[1152,256]{1,0:T(8,128)(2,1)} %fusion.3), channel_id=1, source_target_pairs={{0,192},{1,577},{192,384},{193,1},{384,576},{385,193},{576,0},{577... | collective-permute-start | bytes 1769480 | tf_op jit(solution)/shard_map/ppermute | solution.py:155
  65.4 8.0 %collective-permute-start.7 = (bf16[4,96,256]{2,1,0:T(8,128)(2,1)S(1)}, bf16[4,96,256]{2,1,0:T(8,128)(2,1)S(1)}, u32[]{:S(2)}, u32[]{:S(2)}) collective-permute-start(bf16[4,96,256]{2,1,0:T(8,128)(2,1)S(1)} %get-tuple-element.10), channel_id=1, source_target_pairs={{0,16},{16,32},{32,48},{48,64},{64,80},{80,96},{96,112},{112,128},... | collective-permute-start | bytes 589832 | tf_op jit(solution)/shard_map/ppermute | solution.py:164
  67.3 7.2 %collective-permute-start.8 = (bf16[4,96,256]{2,1,0:T(8,128)(2,1)S(1)}, bf16[4,96,256]{2,1,0:T(8,128)(2,1)S(1)}, u32[]{:S(2)}, u32[]{:S(2)}) collective-permute-start(bf16[4,96,256]{2,1,0:T(8,128)(2,1)S(1)} %get-tuple-element.11), channel_id=1, source_target_pairs={{0,176},{16,0},{32,16},{48,32},{64,48},{80,64},{96,80},{112,96},{1... | collective-permute-start | bytes 589832 | tf_op jit(solution)/shard_map/ppermute | solution.py:165
  75.4 35.2 %all-to-all-start = ((bf16[64,6,256]{2,1,0:T(8,128)(2,1)}), bf16[64,6,256]{2,1,0:T(8,128)(2,1)S(1)}, u32[]{:S(2)}, u32[]{:S(2)}) async-start(bf16[64,6,256]{2,1,0:T(8,128)(2,1)} %reshape.24), calls=%async_computation | async-start | bytes 524288 | tf_op jit(solution)/shard_map/all_to_all | solution.py:168
  110.6 0.7 copy-start.3
Sparse Core Ops, SparseCore 0:
  37.9 44.9 all-gather.2

commit v3 on v2

--- a/solution.py
+++ b/solution.py
@@ -1,3 +1,5 @@
+import functools
+
 import jax
 import jax.numpy as jnp
 from jax import lax
@@ -82,6 +84,7 @@
         out_shape=jax.ShapeDtypeStruct((NZL * own.shape[0], *own.shape[1:]), BF),
         in_specs=[pl.BlockSpec(memory_space=pltpu.SMEM), vmem, vmem, vmem, pl.BlockSpec(memory_space=pl.ANY)],
         out_specs=vmem,
+        compiler_params=pltpu.CompilerParams(vmem_limit_bytes=60 * 2**20),
         cost_estimate=pl.CostEstimate(flops=0, bytes_accessed=4 * NZL * own.size, transcendentals=0),
     )(zl, own, above, below, after)
 
@@ -113,8 +116,55 @@
     )(terms, master, first, second, after)
 
 
-def dot_t(a, b):
-    return lax.dot_general(a, b, (((0,), (0,)), ((), ())), preferred_element_type=F32)
+def term_kernel(plan, where, tokens, theirs, cot, cot_theirs, after, *rest):
+    outs, (lhs, rhs, sems) = rest[: len(plan)], rest[len(plan) :]
+    rows, chunk = lhs.shape[1] // 2, lhs.shape[2]
+    half = outs[0].shape[1]
+    chunks = sorted({p[0] for p in plan})
+
+    def copies(k):
+        columns = pl.ds(pl.multiple_of(where[chunks[k]] * chunk, 128), chunk)
+        return [
+            pltpu.make_async_copy(source.at[:, columns], lhs.at[k, pl.ds(d * rows, rows)], sems.at[k, d])
+            for d, source in enumerate((tokens, theirs))
+        ]
+
+    for k in range(len(chunks)):
+        for copy in copies(k):
+            copy.start()
+    arrived = set()
+    for out, (which, side, kind) in zip(outs, plan):
+        columns = pl.ds(pl.multiple_of(where[side] * half, 128), half)
+        rhs[:rows] = cot[:, columns]
+        rhs[rows:] = cot_theirs[:, columns]
+        k = chunks.index(which)
+        if k not in arrived:
+            arrived.add(k)
+            for copy in copies(k):
+                copy.wait()
+        value = lax.dot_general(lhs[k], rhs[...], (((0,), (0,)), ((), ())), preferred_element_type=F32)
+        out[...] = value.astype(kind)
+
+
+def terms(plan, where, tokens, theirs, cot, cot_theirs, after):
+    rows, chunk, half = tokens.shape[0], tokens.shape[1] // NX, cot.shape[1] // 2
+    vmem, hbm = pl.BlockSpec(memory_space=pltpu.VMEM), pl.BlockSpec(memory_space=pl.ANY)
+    count = len({p[0] for p in plan})
+    return pl.pallas_call(
+        functools.partial(term_kernel, plan),
+        out_shape=[jax.ShapeDtypeStruct((chunk, half), p[2]) for p in plan],
+        in_specs=[pl.BlockSpec(memory_space=pltpu.SMEM), hbm, hbm, vmem, vmem, hbm],
+        out_specs=[vmem] * len(plan),
+        scratch_shapes=[
+            pltpu.VMEM((count, 2 * rows, chunk), BF),
+            pltpu.VMEM((2 * rows, half), BF),
+            pltpu.SemaphoreType.DMA((count, 2)),
+        ],
+        compiler_params=pltpu.CompilerParams(vmem_limit_bytes=60 * 2**20),
+        cost_estimate=pl.CostEstimate(
+            flops=4 * rows * chunk * half * len(plan), bytes_accessed=4 * rows * chunk * count, transcendentals=0
+        ),
+    )(where, tokens, theirs, cot, cot_theirs, after)
 
 
 def local(tokens, cot, codes, scales, master, first, second):
@@ -135,25 +185,20 @@
     chunk, half = width // NX, columns // 2
     on = x + 1 + 2 * c
 
-    def part(k, j):
-        return lax.dynamic_slice_in_dim(k, (j & (NX - 1)) * chunk, chunk, axis=1)
-
-    near = [lax.dynamic_slice_in_dim(k, c * half, half, axis=1) for k in (cot, cot_theirs)]
-    far = [lax.dynamic_slice_in_dim(k, (1 - c) * half, half, axis=1) for k in (cot, cot_theirs)]
-
-    def term(j, cots):
-        return dot_t(part(tokens, j), cots[0]) + dot_t(part(theirs, j), cots[1])
-
+    where = jnp.stack([(x + 2) & (NX - 1), on & (NX - 1), x, c, 1 - c]).astype(jnp.int32)
+    both = (where, tokens, theirs, cot, cot_theirs)
+    TWO, ONE, HERE, NEAR, FAR = range(5)
     straight = [(2 * i + d, 2 * ((i + 1 - 2 * d) % NX) + d) for i in range(NX) for d in range(2)]
     crossed = [(2 * i + d, 2 * ((i + 1 - 2 * d) % NX) + 1 - d) for i in range(NX) for d in range(2)]
-    two_on = term(x + 2, near).astype(BF)
+    (two_on,) = terms([(TWO, NEAR, BF)], *both, cot)
     tiles = in_z_order(zl.astype(jnp.int32).reshape(1), w, above, below, two_on)
     tiles = lax.all_gather(tiles, ("y", "c"), axis=0)
+    (one_far,) = terms([(ONE, FAR, BF)], *both, two_on)
+    one_near, here = terms([(ONE, NEAR, F32), (HERE, NEAR, F32)], *both, one_far)
     two_on = lax.ppermute(two_on, ("x", "c"), straight)
-    one_far = lax.ppermute(term(on, far).astype(BF), ("x", "c"), crossed)
-    one_near = (term(on, near) + two_on.astype(F32)).astype(BF)
-    one_near = lax.ppermute(one_near, ("x", "c"), straight)
-    summed = (term(x, near) + one_far.astype(F32) + one_near.astype(F32)).astype(BF)
+    one_far = lax.ppermute(one_far, ("x", "c"), crossed)
+    one_near = lax.ppermute((one_near + two_on.astype(F32)).astype(BF), ("x", "c"), straight)
+    summed = (here + one_far.astype(F32) + one_near.astype(F32)).astype(BF)
 
     rows = chunk // (nz * NY)
     thirds = summed.reshape(NZH, NZL, NY * rows, half)

time: 120 us -> 119 us (level); the launches traced: 120 us -> 117 us
  Pallas kernels: 9.04 us -> 21.3 us
  matrix products: 11.5 us -> 0 us
  starting transfers between devices: 57.3 us -> 52.8 us
  waiting for transfers between devices: 23.9 us -> 20.8 us
  local copies, waits for them, and re-layouts: 1.52 us -> 4.4 us
  other arithmetic: 2.31 us -> 3.85 us
    pallas_call x0 -> x3, Pallas kernels: none -> 12.3 us  [terms(): pl.pallas_call(functools.partial(term_kernel, plan), out_shape=[jax.Shape...]
    dot_general x8 -> x0, matrix products: 11.5 us -> none  [dot_t(): lax.dot_general(a, b, (((0,), (0,)), ((), ())), preferred_element_type=F32)]
    all_to_all x1, waiting for transfers between devices: 13.5 us -> 9.66 us  [local(): last = lax.all_to_all(last, ('zh', 'y', 'c'), 0, 0, tiled=True)]
    unnamed x8 -> x16, local copies, waits for them, and re-layouts: 0.7 us -> 3.51 us
    ppermute x2, starting transfers between devices: 8.79 us -> 6.23 us  [the longest x1 3.18 us: local(): lax.ppermute((one_near + two_on.astype(F32)).astype(BF), ('x', 'c'), stra...]
    all_to_all x1, starting transfers between devices: 16.1 us -> 13.8 us  [local(): last = lax.all_to_all(last, ('zh', 'y', 'c'), 0, 0, tiled=True)]
    convert_element_type x0 -> x3, other arithmetic: none -> 2.18 us  [the longest x1 1.49 us: local(): (one_near + two_on.astype(F32)).astype(BF)]
  transfers between devices with their start and end apart: 11 -> 11, of which waited for: 6 -> 5; matrix products, arithmetic and copies ran while one was open for 12% -> 4% of each run, Pallas kernels for 5% -> 15%
where the time goes in v3:
time: 119 us; the launch traced here: 117 us
  starting transfers between devices  52.8 us (44%)
  Pallas kernels  21.3 us (18%)
  waiting for transfers between devices  20.8 us (17%)
  between operations  14.3 us (12%)
  local copies, waits for them, and re-layouts  4.4 us (4%)
  other arithmetic  3.85 us (3%)
    all_to_all x1, starting transfers between devices, local(): last = lax.all_to_all(last, ('zh', 'y', 'c'), 0, 0, tiled=True)  13.8 us
    ppermute x1, starting transfers between devices, local(): theirs = lax.ppermute(tokens, 'c', swap)  12.4 us
    pallas_call x3, Pallas kernels, terms(): pl.pallas_call(functools.partial(term_kernel, plan), out_shape=[jax.Shape...  12.3 us
    all_to_all x1, waiting for transfers between devices, local(): last = lax.all_to_all(last, ('zh', 'y', 'c'), 0, 0, tiled=True)  9.66 us
    ppermute x1, waiting for transfers between devices, local(): lax.ppermute((one_near + two_on.astype(F32)).astype(BF), ('x', 'c'), stra...  7.58 us
    pallas_call x1, Pallas kernels, project(): pl.pallas_call(project_kernel, out_shape=jax.ShapeDtypeStruct((rows, colu...  5.66 us
    ppermute x1, starting transfers between devices, local(): above = lax.ppermute(w, ('zh', 'zl'), z_down)  5.29 us
    ppermute x1, starting transfers between devices, local(): down = lax.ppermute(third(zl + 2), ('zh', 'zl'), z_down)  4.85 us
  transfers between devices with their start and end apart: 11, of which 5 were waited for; matrix products, arithmetic and copies ran while one was open for 4% of the time, Pallas kernels for 15%

profile of v3, /device:TPU:1, one launch (start us, length us, event | category | flops | bytes accessed | tf_op | source)
XLA Modules:
  0.0 117.4 jit_solution(17223303340941206501)
XLA Ops:
  7.2 12.4 %collective-permute-start.2 = (bf16[256,4608]{1,0:T(8,128)(2,1)}, bf16[256,4608]{1,0:T(8,128)(2,1)S(1)}, u32[]{:S(2)}, u32[]{:S(2)}) collective-permute-start(bf16[256,4608]{1,0:T(8,128)(2,1)} %tokens.5), channel_id=1, source_target_pairs={{0,1},{1,0},{2,3},{3,2},{4,5},{5,4},{6,7},{7,6},{8,9},{9,8},{10,11... | collective-permute-start | bytes 7077896 | tf_op jit(solution)/shard_map/ppermute | solution.py:178
  19.6 1.9 %collective-permute-start.3 = (bf16[256,512]{1,0:T(8,128)(2,1)}, bf16[256,512]{1,0:T(8,128)(2,1)S(1)}, u32[]{:S(2)}, u32[]{:S(2)}) collective-permute-start(bf16[256,512]{1,0:T(8,128)(2,1)} %cot.5), channel_id=1, source_target_pairs={{0,1},{1,0},{2,3},{3,2},{4,5},{5,4},{6,7},{7,6},{8,9},{9,8},{10,11... | collective-permute-start | bytes 786440 | tf_op jit(solution)/shard_map/ppermute | solution.py:179
  21.6 0.7 bitcast_convert_fusion
  22.3 0.9 multiply_convert_fusion.own
  23.2 5.3 %collective-permute-start = (bf16[3,128,128]{2,1,0:T(8,128)(2,1)S(1)}, bf16[3,128,128]{2,1,0:T(8,128)(2,1)S(1)}, u32[]{:S(2)}, u32[]{:S(2)}) collective-permute-start(bf16[3,128,128]{2,1,0:T(8,128)(2,1)S(1)} %multiply_convert_fusion.own), channel_id=1, source_target_pairs={{0,176},{16,0},{32,16},{48,32},{64,48},{80,64},{96,80},{112,96},{1... | collective-permute-start | bytes 294920 | tf_op jit(solution)/shard_map/ppermute | solution.py:183
  28.5 1.9 %collective-permute-start.1 = (bf16[3,128,128]{2,1,0:T(8,128)(2,1)S(1)}, bf16[3,128,128]{2,1,0:T(8,128)(2,1)S(1)}, u32[]{:S(2)}, u32[]{:S(2)}) collective-permute-start(bf16[3,128,128]{2,1,0:T(8,128)(2,1)S(1)} %multiply_convert_fusion.own), channel_id=1, source_target_pairs={{0,16},{16,32},{32,48},{48,64},{64,80},{80,96},{96,112},{112,128},... | collective-permute-start | bytes 294920 | tf_op jit(solution)/shard_map/ppermute | solution.py:182
  30.4 0.1 stack.23
  30.5 0.5 convert_element_type.58.where
  31.0 0.7 copy-done.2
  31.7 1.4 %copy-done = bf16[256,4608]{1,0:T(8,128)(2,1)} copy-done((bf16[256,4608]{1,0:T(8,128)(2,1)}, bf16[256,4608]{1,0:T(8,128)(2,1)S(1)}, u32[]{:S(2)}) %copy-start) | copy-done | bytes 2359320
  33.2 3.6 %shard_map.102.after = bf16[1152,256]{1,0:T(8,128)(2,1)} custom-call(s32[5]{0:T(128)} %convert_element_type.58.where, bf16[256,4608]{1,0:T(8,128)(2,1)} %tokens.5, bf16[256,4608]{1,0:T(8,128)(2,1)} %copy-done, bf16[256,512]{1,0:T(8,128)(2,1)} %cot.5, bf16[256,512]{1,0:T(8,128)(2,1)} %copy-done.2, bf16[256,512]{1,0:T(8,128)(2,1)} %cot.5), custom_call_target="tpu_custom_call" | custom-call | flops 301989888 | bytes 1179648 | tf_op jit(solution)/shard_map/pallas_call | solution.py:153
  36.9 0.6 copy-done.6
  37.5 1.7 %shard_map.103 = bf16[9,128,128]{2,1,0:T(8,128)(2,1)} custom-call(s32[1]{0:T(128)} %bitcast.zl_ref, bf16[3,128,128]{2,1,0:T(8,128)(2,1)} %copy-done.5, bf16[3,128,128]{2,1,0:T(8,128)(2,1)} %copy-done.6, bf16[3,128,128]{2,1,0:T(8,128)(2,1)} %copy-done.7, bf16[1152,256]{1,0:T(8,128)(2,1)} %shard_map.102.after), custom_call_target="tpu_custom_call" | custom-call | bytes 589824 | tf_op jit(solution)/shard_map/pallas_call | solution.py:82
  39.3 4.4 %collective-permute-start.5 = (bf16[1152,256]{1,0:T(8,128)(2,1)S(1)}, bf16[1152,256]{1,0:T(8,128)(2,1)S(1)}, u32[]{:S(2)}, u32[]{:S(2)}) collective-permute-start(bf16[1152,256]{1,0:T(8,128)(2,1)S(1)} %copy-done.1), channel_id=1, source_target_pairs={{0,192},{1,577},{192,384},{193,1},{384,576},{385,193},{576,0},{577... | collective-permute-start | bytes 1769480 | tf_op jit(solution)/shard_map/ppermute | solution.py:198
  43.7 3.6 %shard_map.105.after = bf16[1152,256]{1,0:T(8,128)(2,1)} custom-call(s32[5]{0:T(128)} %convert_element_type.58.where, bf16[256,4608]{1,0:T(8,128)(2,1)} %tokens.5, bf16[256,4608]{1,0:T(8,128)(2,1)} %copy-done, bf16[256,512]{1,0:T(8,128)(2,1)} %cot.5, bf16[256,512]{1,0:T(8,128)(2,1)} %copy-done.2, bf16[1152,256]{1,0:T(8,128)(2,1)} %shard_map.102.after), custom_call_target="tpu_custom_call" | custom-call | flops 301989888 | bytes 1179648 | tf_op jit(solution)/shard_map/pallas_call | solution.py:153
  47.4 3.1 %collective-permute-start.4 = (bf16[1152,256]{1,0:T(8,128)(2,1)}, bf16[1152,256]{1,0:T(8,128)(2,1)S(1)}, u32[]{:S(2)}, u32[]{:S(2)}) collective-permute-start(bf16[1152,256]{1,0:T(8,128)(2,1)} %shard_map.105.after), channel_id=1, source_target_pairs={{0,193},{1,576},{192,385},{193,0},{384,577},{385,192},{576,1},{577... | collective-permute-start | bytes 1769480 | tf_op jit(solution)/shard_map/ppermute | solution.py:199
  50.4 5.0 %shard_map.106 = (f32[1152,256]{1,0:T(8,128)}, f32[1152,256]{1,0:T(8,128)}) custom-call(s32[5]{0:T(128)} %convert_element_type.58.where, bf16[256,4608]{1,0:T(8,128)(2,1)} %tokens.5, bf16[256,4608]{1,0:T(8,128)(2,1)} %copy-done, bf16[256,512]{1,0:T(8,128)(2,1)} %cot.5, bf16[256,512]{1,0:T(8,128)(2,1)} %copy-done.2, bf16[1152,256]{1,0:T(8,128)(2,1)} %shard_map.105.after), custom_call_target="tpu_custom_call" | custom-call | flops 603979776 | bytes 2359296 | tf_op jit(solution)/shard_map/pallas_call | solution.py:153
  55.4 1.5 %add_convert_fusion.1 = bf16[1152,256]{1,0:T(8,128)(2,1)S(1)} fusion(f32[1152,256]{1,0:T(8,128)} %get-tuple-element.10, bf16[1152,256]{1,0:T(8,128)(2,1)S(1)} %collective-permute-done.5), kind=kLoop, calls=%fused_computation.1 | loop fusion | flops 884736 | bytes 2359296 | tf_op jit(solution)/shard_map/convert_element_type | solution.py:200
  56.9 3.2 %collective-permute-start.6 = (bf16[1152,256]{1,0:T(8,128)(2,1)S(1)}, bf16[1152,256]{1,0:T(8,128)(2,1)S(1)}, u32[]{:S(2)}, u32[]{:S(2)}) collective-permute-start(bf16[1152,256]{1,0:T(8,128)(2,1)S(1)} %add_convert_fusion.1), channel_id=1, source_target_pairs={{0,192},{1,577},{192,384},{193,1},{384,576},{385,193},{576,0},{577... | collective-permute-start | bytes 1769480 | tf_op jit(solution)/shard_map/ppermute | solution.py:200
  60.1 0.3 collective-permute-done.4
  60.4 7.6 %collective-permute-done.6 = bf16[1152,256]{1,0:T(8,128)(2,1)S(1)} collective-permute-done((bf16[1152,256]{1,0:T(8,128)(2,1)S(1)}, bf16[1152,256]{1,0:T(8,128)(2,1)S(1)}, u32[]{:S(2)}, u32[]{:S(2)}) %collective-permute-start.6) | collective-permute-done | bytes 589856 | tf_op jit(solution)/shard_map/ppermute | solution.py:200
  68.0 0.2 add_convert_fusion
  68.2 1.9 %collective-permute-start.7 = (bf16[4,96,256]{2,1,0:T(8,128)(2,1)S(1)}, bf16[4,96,256]{2,1,0:T(8,128)(2,1)S(1)}, u32[]{:S(2)}, u32[]{:S(2)}) collective-permute-start(bf16[4,96,256]{2,1,0:T(8,128)(2,1)S(1)} %get-tuple-element.14), channel_id=1, source_target_pairs={{0,16},{16,32},{32,48},{48,64},{64,80},{80,96},{96,112},{112,128},... | collective-permute-start | bytes 589832 | tf_op jit(solution)/shard_map/ppermute | solution.py:209
  70.1 4.9 %collective-permute-start.8 = (bf16[4,96,256]{2,1,0:T(8,128)(2,1)S(1)}, bf16[4,96,256]{2,1,0:T(8,128)(2,1)S(1)}, u32[]{:S(2)}, u32[]{:S(2)}) collective-permute-start(bf16[4,96,256]{2,1,0:T(8,128)(2,1)S(1)} %get-tuple-element.15), channel_id=1, source_target_pairs={{0,176},{16,0},{32,16},{48,32},{64,48},{80,64},{96,80},{112,96},{1... | collective-permute-start | bytes 589832 | tf_op jit(solution)/shard_map/ppermute | solution.py:210
  75.0 2.4 %collective-permute-done.7 = bf16[4,96,256]{2,1,0:T(8,128)(2,1)S(1)} collective-permute-done((bf16[4,96,256]{2,1,0:T(8,128)(2,1)S(1)}, bf16[4,96,256]{2,1,0:T(8,128)(2,1)S(1)}, u32[]{:S(2)}, u32[]{:S(2)}) %collective-permute-start.7) | collective-permute-done | bytes 196640 | tf_op jit(solution)/shard_map/ppermute | solution.py:209
  77.3 0.9 collective-permute-done.8
  78.3 0.8 reshape.24
  79.0 13.8 %all-to-all-start = ((bf16[64,6,256]{2,1,0:T(8,128)(2,1)}), bf16[64,6,256]{2,1,0:T(8,128)(2,1)S(1)}, u32[]{:S(2)}, u32[]{:S(2)}) async-start(bf16[64,6,256]{2,1,0:T(8,128)(2,1)} %reshape.24), calls=%async_computation | async-start | bytes 524288 | tf_op jit(solution)/shard_map/all_to_all | solution.py:213
  92.9 5.7 %shard_map.104.after = bf16[256,512]{1,0:T(8,128)(2,1)} custom-call(bf16[256,4608]{1,0:T(8,128)(2,1)} %tokens.5, bf16[16,9,128,128]{3,2,1,0:T(8,128)(2,1)} %bitcast.21), custom_call_target="tpu_custom_call" | custom-call | flops 1207959552 | bytes 7077888 | tf_op jit(solution)/shard_map/pallas_call | solution.py:54
  98.5 9.7 %all-to-all-done = bf16[64,6,256]{2,1,0:T(8,128)(2,1)S(1)} async-done(((bf16[64,6,256]{2,1,0:T(8,128)(2,1)}), bf16[64,6,256]{2,1,0:T(8,128)(2,1)S(1)}, u32[]{:S(2)}, u32[]{:S(2)}) %all-to-all-start) | async-done | bytes 196640 | tf_op jit(solution)/shard_map/all_to_all | solution.py:213
  108.2 0.7 copy-done.4
  108.9 1.7 %shard_map.107 = (f32[6,512]{1,0:T(8,128)}, f32[6,512]{1,0:T(8,128)}, f32[6,512]{1,0:T(8,128)}) custom-call(bf16[32,2,6,256]{3,2,1,0:T(8,128)(2,1)} %bitcast.24, f32[6,512]{1,0:T(8,128)} %master.1, f32[6,512]{1,0:T(8,128)} %first.1, f32[6,512]{1,0:T(8,128)} %second.1, bf16[256,512]{1,0:T(8,128)(2,1)} %shard_map.104.after), custom_call_target="tpu_custom_call" | custom-call | flops 61440 | bytes 270336 | tf_op jit(solution)/shard_map/pallas_call | solution.py:110
  (22 shorter events, 0.3 us)
Async XLA Ops:
  7.2 85.7 %all-gather.3.cloned.1.call-start = ((), (), s32[]{:S(2)}) async-start(), calls=%async_computation.1 | async-start | bytes 5013504 | tf_op jit(solution)/shard_map/all_gather | solution.py:195
  7.2 23.8 %collective-permute-start.2 = (bf16[256,4608]{1,0:T(8,128)(2,1)}, bf16[256,4608]{1,0:T(8,128)(2,1)S(1)}, u32[]{:S(2)}, u32[]{:S(2)}) collective-permute-start(bf16[256,4608]{1,0:T(8,128)(2,1)} %tokens.5), channel_id=1, source_target_pairs={{0,1},{1,0},{2,3},{3,2},{4,5},{5,4},{6,7},{7,6},{8,9},{9,8},{10,11... | collective-permute-start | bytes 7077896 | tf_op jit(solution)/shard_map/ppermute | solution.py:178
  19.6 11.4 %collective-permute-start.3 = (bf16[256,512]{1,0:T(8,128)(2,1)}, bf16[256,512]{1,0:T(8,128)(2,1)S(1)}, u32[]{:S(2)}, u32[]{:S(2)}) collective-permute-start(bf16[256,512]{1,0:T(8,128)(2,1)} %cot.5), channel_id=1, source_target_pairs={{0,1},{1,0},{2,3},{3,2},{4,5},{5,4},{6,7},{7,6},{8,9},{9,8},{10,11... | collective-permute-start | bytes 786440 | tf_op jit(solution)/shard_map/ppermute | solution.py:179
  23.2 13.7 %copy-start.5 = (bf16[3,128,128]{2,1,0:T(8,128)(2,1)}, bf16[3,128,128]{2,1,0:T(8,128)(2,1)S(1)}, u32[]{:S(2)}) copy-start(bf16[3,128,128]{2,1,0:T(8,128)(2,1)S(1)} %multiply_convert_fusion.own) | copy-start | bytes 294916
  23.2 13.6 %collective-permute-start = (bf16[3,128,128]{2,1,0:T(8,128)(2,1)S(1)}, bf16[3,128,128]{2,1,0:T(8,128)(2,1)S(1)}, u32[]{:S(2)}, u32[]{:S(2)}) collective-permute-start(bf16[3,128,128]{2,1,0:T(8,128)(2,1)S(1)} %multiply_convert_fusion.own), channel_id=1, source_target_pairs={{0,176},{16,0},{32,16},{48,32},{64,48},{80,64},{96,80},{112,96},{1... | collective-permute-start | bytes 294920 | tf_op jit(solution)/shard_map/ppermute | solution.py:183
  28.5 8.4 %collective-permute-start.1 = (bf16[3,128,128]{2,1,0:T(8,128)(2,1)S(1)}, bf16[3,128,128]{2,1,0:T(8,128)(2,1)S(1)}, u32[]{:S(2)}, u32[]{:S(2)}) collective-permute-start(bf16[3,128,128]{2,1,0:T(8,128)(2,1)S(1)} %multiply_convert_fusion.own), channel_id=1, source_target_pairs={{0,16},{16,32},{32,48},{48,64},{64,80},{80,96},{96,112},{112,128},... | collective-permute-start | bytes 294920 | tf_op jit(solution)/shard_map/ppermute | solution.py:182
  31.0 0.7 copy-start.2
  31.7 1.4 %copy-start = (bf16[256,4608]{1,0:T(8,128)(2,1)}, bf16[256,4608]{1,0:T(8,128)(2,1)S(1)}, u32[]{:S(2)}) copy-start(bf16[256,4608]{1,0:T(8,128)(2,1)S(1)} %collective-permute-done.2.theirs) | copy-start | bytes 7077892
  36.8 2.5 %copy-start.1 = (bf16[1152,256]{1,0:T(8,128)(2,1)S(1)}, bf16[1152,256]{1,0:T(8,128)(2,1)}, u32[]{:S(2)}) copy-start(bf16[1152,256]{1,0:T(8,128)(2,1)} %shard_map.102.after) | copy-start | bytes 1769476
  36.8 0.6 copy-start.6
  36.9 0.7 copy-start.7
  39.3 16.1 %collective-permute-start.5 = (bf16[1152,256]{1,0:T(8,128)(2,1)S(1)}, bf16[1152,256]{1,0:T(8,128)(2,1)S(1)}, u32[]{:S(2)}, u32[]{:S(2)}) collective-permute-start(bf16[1152,256]{1,0:T(8,128)(2,1)S(1)} %copy-done.1), channel_id=1, source_target_pairs={{0,192},{1,577},{192,384},{193,1},{384,576},{385,193},{576,0},{577... | collective-permute-start | bytes 1769480 | tf_op jit(solution)/shard_map/ppermute | solution.py:198
  47.4 13.0 %collective-permute-start.4 = (bf16[1152,256]{1,0:T(8,128)(2,1)}, bf16[1152,256]{1,0:T(8,128)(2,1)S(1)}, u32[]{:S(2)}, u32[]{:S(2)}) collective-permute-start(bf16[1152,256]{1,0:T(8,128)(2,1)} %shard_map.105.after), channel_id=1, source_target_pairs={{0,193},{1,576},{192,385},{193,0},{384,577},{385,192},{576,1},{577... | collective-permute-start | bytes 1769480 | tf_op jit(solution)/shard_map/ppermute | solution.py:199
  55.4 12.5 %copy-start.3 = (f32[1152,256]{1,0:T(8,128)S(1)}, f32[1152,256]{1,0:T(8,128)}, u32[]{:S(2)}) copy-start(f32[1152,256]{1,0:T(8,128)} %get-tuple-element.9) | copy-start | bytes 3538948
  56.9 11.0 %collective-permute-start.6 = (bf16[1152,256]{1,0:T(8,128)(2,1)S(1)}, bf16[1152,256]{1,0:T(8,128)(2,1)S(1)}, u32[]{:S(2)}, u32[]{:S(2)}) collective-permute-start(bf16[1152,256]{1,0:T(8,128)(2,1)S(1)} %add_convert_fusion.1), channel_id=1, source_target_pairs={{0,192},{1,577},{192,384},{193,1},{384,576},{385,193},{576,0},{577... | collective-permute-start | bytes 1769480 | tf_op jit(solution)/shard_map/ppermute | solution.py:200
  68.2 9.2 %collective-permute-start.7 = (bf16[4,96,256]{2,1,0:T(8,128)(2,1)S(1)}, bf16[4,96,256]{2,1,0:T(8,128)(2,1)S(1)}, u32[]{:S(2)}, u32[]{:S(2)}) collective-permute-start(bf16[4,96,256]{2,1,0:T(8,128)(2,1)S(1)} %get-tuple-element.14), channel_id=1, source_target_pairs={{0,16},{16,32},{32,48},{48,64},{64,80},{80,96},{96,112},{112,128},... | collective-permute-start | bytes 589832 | tf_op jit(solution)/shard_map/ppermute | solution.py:209
  70.1 8.1 %collective-permute-start.8 = (bf16[4,96,256]{2,1,0:T(8,128)(2,1)S(1)}, bf16[4,96,256]{2,1,0:T(8,128)(2,1)S(1)}, u32[]{:S(2)}, u32[]{:S(2)}) collective-permute-start(bf16[4,96,256]{2,1,0:T(8,128)(2,1)S(1)} %get-tuple-element.15), channel_id=1, source_target_pairs={{0,176},{16,0},{32,16},{48,32},{64,48},{80,64},{96,80},{112,96},{1... | collective-permute-start | bytes 589832 | tf_op jit(solution)/shard_map/ppermute | solution.py:210
  79.0 29.1 %all-to-all-start = ((bf16[64,6,256]{2,1,0:T(8,128)(2,1)}), bf16[64,6,256]{2,1,0:T(8,128)(2,1)S(1)}, u32[]{:S(2)}, u32[]{:S(2)}) async-start(bf16[64,6,256]{2,1,0:T(8,128)(2,1)} %reshape.24), calls=%async_computation | async-start | bytes 524288 | tf_op jit(solution)/shard_map/all_to_all | solution.py:213
  108.2 0.7 copy-start.4
Sparse Core Ops, SparseCore 0:
  39.4 45.8 all-gather.2

commit v4 on v3

--- a/solution.py
+++ b/solution.py
@@ -194,10 +194,12 @@
     tiles = in_z_order(zl.astype(jnp.int32).reshape(1), w, above, below, two_on)
     tiles = lax.all_gather(tiles, ("y", "c"), axis=0)
     (one_far,) = terms([(ONE, FAR, BF)], *both, two_on)
-    one_near, here = terms([(ONE, NEAR, F32), (HERE, NEAR, F32)], *both, one_far)
+    (one_near,) = terms([(ONE, NEAR, F32)], *both, one_far)
     two_on = lax.ppermute(two_on, ("x", "c"), straight)
     one_far = lax.ppermute(one_far, ("x", "c"), crossed)
-    one_near = lax.ppermute((one_near + two_on.astype(F32)).astype(BF), ("x", "c"), straight)
+    one_near = (one_near + two_on.astype(F32)).astype(BF)
+    (here,) = terms([(HERE, NEAR, F32)], *both, one_near)
+    one_near = lax.ppermute(one_near, ("x", "c"), straight)
     summed = (here + one_far.astype(F32) + one_near.astype(F32)).astype(BF)
 
     rows = chunk // (nz * NY)

time: 119 us -> 119 us (level)
  waiting for transfers between devices: 20.8 us -> 16.6 us
  Pallas kernels: 21.3 us -> 24.2 us
    ppermute x1, waiting for transfers between devices: 7.58 us -> 3.68 us  [local(): one_near = lax.ppermute(one_near, ('x', 'c'), straight)]
    pallas_call x3 -> x4, Pallas kernels: 12.3 us -> 15.2 us  [terms(): pl.pallas_call(functools.partial(term_kernel, plan), out_shape=[jax.Shape...]
    convert_element_type x1, other arithmetic: 0.18 us -> 1.45 us  [local(): summed = (here + one_far.astype(F32) + one_near.astype(F32)).astype(BF)]
  transfers between devices with their start and end apart: 11 -> 11, of which waited for: 5 -> 4; matrix products, arithmetic and copies ran while one was open for 4% -> 5% of each run, Pallas kernels for 15% -> 18%
where the time goes in v4:
time: 119 us; the launch traced here: 118 us
  starting transfers between devices  53 us (45%)
  Pallas kernels  24.2 us (20%)
  waiting for transfers between devices  16.6 us (14%)
  between operations  14.3 us (12%)
  other arithmetic  5.03 us (4%)
  local copies, waits for them, and re-layouts  4.38 us (4%)
    pallas_call x4, Pallas kernels, terms(): pl.pallas_call(functools.partial(term_kernel, plan), out_shape=[jax.Shape...  15.2 us
    all_to_all x1, starting transfers between devices, local(): last = lax.all_to_all(last, ('zh', 'y', 'c'), 0, 0, tiled=True)  13.8 us
    ppermute x1, starting transfers between devices, local(): theirs = lax.ppermute(tokens, 'c', swap)  12.4 us
    all_to_all x1, waiting for transfers between devices, local(): last = lax.all_to_all(last, ('zh', 'y', 'c'), 0, 0, tiled=True)  9.68 us
    pallas_call x1, Pallas kernels, project(): pl.pallas_call(project_kernel, out_shape=jax.ShapeDtypeStruct((rows, colu...  5.67 us
    ppermute x1, starting transfers between devices, local(): above = lax.ppermute(w, ('zh', 'zl'), z_down)  5.29 us
    ppermute x1, starting transfers between devices, local(): down = lax.ppermute(third(zl + 2), ('zh', 'zl'), z_down)  4.88 us
    ppermute x1, starting transfers between devices, local(): two_on = lax.ppermute(two_on, ('x', 'c'), straight)  4.39 us
  transfers between devices with their start and end apart: 11, of which 4 were waited for; matrix products, arithmetic and copies ran while one was open for 5% of the time, Pallas kernels for 18%

profile of v4, /device:TPU:1, one launch (start us, length us, event | category | flops | bytes accessed | tf_op | source)
XLA Modules:
  0.0 117.6 jit_solution(9025027522560517774)
XLA Ops:
  7.2 12.4 %collective-permute-start.2 = (bf16[256,4608]{1,0:T(8,128)(2,1)}, bf16[256,4608]{1,0:T(8,128)(2,1)S(1)}, u32[]{:S(2)}, u32[]{:S(2)}) collective-permute-start(bf16[256,4608]{1,0:T(8,128)(2,1)} %tokens.7), channel_id=1, source_target_pairs={{0,1},{1,0},{2,3},{3,2},{4,5},{5,4},{6,7},{7,6},{8,9},{9,8},{10,11... | collective-permute-start | bytes 7077896 | tf_op jit(solution)/shard_map/ppermute | solution.py:178
  19.6 1.9 %collective-permute-start.3 = (bf16[256,512]{1,0:T(8,128)(2,1)}, bf16[256,512]{1,0:T(8,128)(2,1)S(1)}, u32[]{:S(2)}, u32[]{:S(2)}) collective-permute-start(bf16[256,512]{1,0:T(8,128)(2,1)} %cot.7), channel_id=1, source_target_pairs={{0,1},{1,0},{2,3},{3,2},{4,5},{5,4},{6,7},{7,6},{8,9},{9,8},{10,11... | collective-permute-start | bytes 786440 | tf_op jit(solution)/shard_map/ppermute | solution.py:179
  21.6 0.7 bitcast_convert_fusion
  22.3 0.9 multiply_convert_fusion.own
  23.2 5.3 %collective-permute-start = (bf16[3,128,128]{2,1,0:T(8,128)(2,1)S(1)}, bf16[3,128,128]{2,1,0:T(8,128)(2,1)S(1)}, u32[]{:S(2)}, u32[]{:S(2)}) collective-permute-start(bf16[3,128,128]{2,1,0:T(8,128)(2,1)S(1)} %multiply_convert_fusion.own), channel_id=1, source_target_pairs={{0,176},{16,0},{32,16},{48,32},{64,48},{80,64},{96,80},{112,96},{1... | collective-permute-start | bytes 294920 | tf_op jit(solution)/shard_map/ppermute | solution.py:183
  28.5 1.9 %collective-permute-start.1 = (bf16[3,128,128]{2,1,0:T(8,128)(2,1)S(1)}, bf16[3,128,128]{2,1,0:T(8,128)(2,1)S(1)}, u32[]{:S(2)}, u32[]{:S(2)}) collective-permute-start(bf16[3,128,128]{2,1,0:T(8,128)(2,1)S(1)} %multiply_convert_fusion.own), channel_id=1, source_target_pairs={{0,16},{16,32},{32,48},{48,64},{64,80},{80,96},{96,112},{112,128},... | collective-permute-start | bytes 294920 | tf_op jit(solution)/shard_map/ppermute | solution.py:182
  30.4 0.1 stack.23
  30.5 0.5 convert_element_type.58.where
  31.0 0.7 copy-done.2
  31.7 1.4 %copy-done = bf16[256,4608]{1,0:T(8,128)(2,1)} copy-done((bf16[256,4608]{1,0:T(8,128)(2,1)}, bf16[256,4608]{1,0:T(8,128)(2,1)S(1)}, u32[]{:S(2)}) %copy-start) | copy-done | bytes 2359320
  33.2 3.6 %shard_map.102.after = bf16[1152,256]{1,0:T(8,128)(2,1)} custom-call(s32[5]{0:T(128)} %convert_element_type.58.where, bf16[256,4608]{1,0:T(8,128)(2,1)} %tokens.7, bf16[256,4608]{1,0:T(8,128)(2,1)} %copy-done, bf16[256,512]{1,0:T(8,128)(2,1)} %cot.7, bf16[256,512]{1,0:T(8,128)(2,1)} %copy-done.2, bf16[256,512]{1,0:T(8,128)(2,1)} %cot.7), custom_call_target="tpu_custom_call" | custom-call | flops 301989888 | bytes 1179648 | tf_op jit(solution)/shard_map/pallas_call | solution.py:153
  36.9 0.6 copy-done.6
  37.5 1.7 %shard_map.103 = bf16[9,128,128]{2,1,0:T(8,128)(2,1)} custom-call(s32[1]{0:T(128)} %bitcast.zl_ref, bf16[3,128,128]{2,1,0:T(8,128)(2,1)} %copy-done.5, bf16[3,128,128]{2,1,0:T(8,128)(2,1)} %copy-done.6, bf16[3,128,128]{2,1,0:T(8,128)(2,1)} %copy-done.7, bf16[1152,256]{1,0:T(8,128)(2,1)} %shard_map.102.after), custom_call_target="tpu_custom_call" | custom-call | bytes 589824 | tf_op jit(solution)/shard_map/pallas_call | solution.py:82
  39.3 4.4 %collective-permute-start.4 = (bf16[1152,256]{1,0:T(8,128)(2,1)S(1)}, bf16[1152,256]{1,0:T(8,128)(2,1)S(1)}, u32[]{:S(2)}, u32[]{:S(2)}) collective-permute-start(bf16[1152,256]{1,0:T(8,128)(2,1)S(1)} %copy-done.1), channel_id=1, source_target_pairs={{0,192},{1,577},{192,384},{193,1},{384,576},{385,193},{576,0},{577... | collective-permute-start | bytes 1769480 | tf_op jit(solution)/shard_map/ppermute | solution.py:198
  43.7 3.7 %shard_map.105.after = bf16[1152,256]{1,0:T(8,128)(2,1)} custom-call(s32[5]{0:T(128)} %convert_element_type.58.where, bf16[256,4608]{1,0:T(8,128)(2,1)} %tokens.7, bf16[256,4608]{1,0:T(8,128)(2,1)} %copy-done, bf16[256,512]{1,0:T(8,128)(2,1)} %cot.7, bf16[256,512]{1,0:T(8,128)(2,1)} %copy-done.2, bf16[1152,256]{1,0:T(8,128)(2,1)} %shard_map.102.after), custom_call_target="tpu_custom_call" | custom-call | flops 301989888 | bytes 1179648 | tf_op jit(solution)/shard_map/pallas_call | solution.py:153
  47.4 3.1 %collective-permute-start.5 = (bf16[1152,256]{1,0:T(8,128)(2,1)}, bf16[1152,256]{1,0:T(8,128)(2,1)S(1)}, u32[]{:S(2)}, u32[]{:S(2)}) collective-permute-start(bf16[1152,256]{1,0:T(8,128)(2,1)} %shard_map.105.after), channel_id=1, source_target_pairs={{0,193},{1,576},{192,385},{193,0},{384,577},{385,192},{576,1},{577... | collective-permute-start | bytes 1769480 | tf_op jit(solution)/shard_map/ppermute | solution.py:199
  50.4 3.9 %shard_map.106 = f32[1152,256]{1,0:T(8,128)} custom-call(s32[5]{0:T(128)} %convert_element_type.58.where, bf16[256,4608]{1,0:T(8,128)(2,1)} %tokens.7, bf16[256,4608]{1,0:T(8,128)(2,1)} %copy-done, bf16[256,512]{1,0:T(8,128)(2,1)} %cot.7, bf16[256,512]{1,0:T(8,128)(2,1)} %copy-done.2, bf16[1152,256]{1,0:T(8,128)(2,1)} %shard_map.105.after), custom_call_target="tpu_custom_call" | custom-call | flops 301989888 | bytes 1179648 | tf_op jit(solution)/shard_map/pallas_call | solution.py:153
  54.3 1.4 %add_convert_fusion.1.after = bf16[1152,256]{1,0:T(8,128)(2,1)S(1)} fusion(f32[1152,256]{1,0:T(8,128)} %shard_map.106, bf16[1152,256]{1,0:T(8,128)(2,1)S(1)} %collective-permute-done.4), kind=kLoop, calls=%fused_computation.1 | loop fusion | flops 884736 | bytes 2359296 | tf_op jit(solution)/shard_map/convert_element_type | solution.py:200
  55.8 3.4 %collective-permute-start.6 = (bf16[1152,256]{1,0:T(8,128)(2,1)S(1)}, bf16[1152,256]{1,0:T(8,128)(2,1)S(1)}, u32[]{:S(2)}, u32[]{:S(2)}) collective-permute-start(bf16[1152,256]{1,0:T(8,128)(2,1)S(1)} %add_convert_fusion.1.after), channel_id=1, source_target_pairs={{0,192},{1,577},{192,384},{193,1},{384,576},{385,193},{576,0},{577... | collective-permute-start | bytes 1769480 | tf_op jit(solution)/shard_map/ppermute | solution.py:202
  59.2 3.9 %shard_map.107 = f32[1152,256]{1,0:T(8,128)} custom-call(s32[5]{0:T(128)} %convert_element_type.58.where, bf16[256,4608]{1,0:T(8,128)(2,1)} %tokens.7, bf16[256,4608]{1,0:T(8,128)(2,1)} %copy-done, bf16[256,512]{1,0:T(8,128)(2,1)} %cot.7, bf16[256,512]{1,0:T(8,128)(2,1)} %copy-done.2, bf16[1152,256]{1,0:T(8,128)(2,1)} %copy-done.3), custom_call_target="tpu_custom_call" | custom-call | flops 301989888 | bytes 1179648 | tf_op jit(solution)/shard_map/pallas_call | solution.py:153
  63.1 3.7 %collective-permute-done.6 = bf16[1152,256]{1,0:T(8,128)(2,1)S(1)} collective-permute-done((bf16[1152,256]{1,0:T(8,128)(2,1)S(1)}, bf16[1152,256]{1,0:T(8,128)(2,1)S(1)}, u32[]{:S(2)}, u32[]{:S(2)}) %collective-permute-start.6) | collective-permute-done | bytes 589856 | tf_op jit(solution)/shard_map/ppermute | solution.py:202
  66.8 1.4 %add_convert_fusion = bf16[1152,256]{1,0:T(8,128)(2,1)S(1)} fusion(bf16[1152,256]{1,0:T(8,128)(2,1)S(1)} %collective-permute-done.6, f32[1152,256]{1,0:T(8,128)} %shard_map.107, bf16[1152,256]{1,0:T(8,128)(2,1)S(1)} %collective-permute-done.5), kind=kLoop, calls=%fused_computation | loop fusion | flops 1474560 | bytes 2949120 | tf_op jit(solution)/shard_map/convert_element_type | solution.py:203
  68.3 1.9 %collective-permute-start.7 = (bf16[4,96,256]{2,1,0:T(8,128)(2,1)S(1)}, bf16[4,96,256]{2,1,0:T(8,128)(2,1)S(1)}, u32[]{:S(2)}, u32[]{:S(2)}) collective-permute-start(bf16[4,96,256]{2,1,0:T(8,128)(2,1)S(1)} %get-tuple-element.10), channel_id=1, source_target_pairs={{0,16},{16,32},{32,48},{48,64},{64,80},{80,96},{96,112},{112,128},... | collective-permute-start | bytes 589832 | tf_op jit(solution)/shard_map/ppermute | solution.py:211
  70.2 4.9 %collective-permute-start.8 = (bf16[4,96,256]{2,1,0:T(8,128)(2,1)S(1)}, bf16[4,96,256]{2,1,0:T(8,128)(2,1)S(1)}, u32[]{:S(2)}, u32[]{:S(2)}) collective-permute-start(bf16[4,96,256]{2,1,0:T(8,128)(2,1)S(1)} %get-tuple-element.11), channel_id=1, source_target_pairs={{0,176},{16,0},{32,16},{48,32},{64,48},{80,64},{96,80},{112,96},{1... | collective-permute-start | bytes 589832 | tf_op jit(solution)/shard_map/ppermute | solution.py:212
  75.1 2.3 %collective-permute-done.7 = bf16[4,96,256]{2,1,0:T(8,128)(2,1)S(1)} collective-permute-done((bf16[4,96,256]{2,1,0:T(8,128)(2,1)S(1)}, bf16[4,96,256]{2,1,0:T(8,128)(2,1)S(1)}, u32[]{:S(2)}, u32[]{:S(2)}) %collective-permute-start.7) | collective-permute-done | bytes 196640 | tf_op jit(solution)/shard_map/ppermute | solution.py:211
  77.4 0.9 collective-permute-done.8
  78.4 0.8 reshape.24
  79.2 13.8 %all-to-all-start = ((bf16[64,6,256]{2,1,0:T(8,128)(2,1)}), bf16[64,6,256]{2,1,0:T(8,128)(2,1)S(1)}, u32[]{:S(2)}, u32[]{:S(2)}) async-start(bf16[64,6,256]{2,1,0:T(8,128)(2,1)} %reshape.24), calls=%async_computation | async-start | bytes 524288 | tf_op jit(solution)/shard_map/all_to_all | solution.py:215
  93.0 5.7 %shard_map.104.after = bf16[256,512]{1,0:T(8,128)(2,1)} custom-call(bf16[256,4608]{1,0:T(8,128)(2,1)} %tokens.7, bf16[16,9,128,128]{3,2,1,0:T(8,128)(2,1)} %bitcast.21), custom_call_target="tpu_custom_call" | custom-call | flops 1207959552 | bytes 7077888 | tf_op jit(solution)/shard_map/pallas_call | solution.py:54
  98.7 9.7 %all-to-all-done = bf16[64,6,256]{2,1,0:T(8,128)(2,1)S(1)} async-done(((bf16[64,6,256]{2,1,0:T(8,128)(2,1)}), bf16[64,6,256]{2,1,0:T(8,128)(2,1)S(1)}, u32[]{:S(2)}, u32[]{:S(2)}) %all-to-all-start) | async-done | bytes 196640 | tf_op jit(solution)/shard_map/all_to_all | solution.py:215
  108.3 0.7 copy-done.4
  109.0 1.7 %shard_map.108 = (f32[6,512]{1,0:T(8,128)}, f32[6,512]{1,0:T(8,128)}, f32[6,512]{1,0:T(8,128)}) custom-call(bf16[32,2,6,256]{3,2,1,0:T(8,128)(2,1)} %bitcast.24, f32[6,512]{1,0:T(8,128)} %master.1, f32[6,512]{1,0:T(8,128)} %first.1, f32[6,512]{1,0:T(8,128)} %second.1, bf16[256,512]{1,0:T(8,128)(2,1)} %shard_map.104.after), custom_call_target="tpu_custom_call" | custom-call | flops 61440 | bytes 270336 | tf_op jit(solution)/shard_map/pallas_call | solution.py:110
  (23 shorter events, 0.3 us)
Async XLA Ops:
  7.2 85.8 %all-gather.3.cloned.1.call-start = ((), (), s32[]{:S(2)}) async-start(), calls=%async_computation.1 | async-start | bytes 5013504 | tf_op jit(solution)/shard_map/all_gather | solution.py:195
  7.2 23.8 %collective-permute-start.2 = (bf16[256,4608]{1,0:T(8,128)(2,1)}, bf16[256,4608]{1,0:T(8,128)(2,1)S(1)}, u32[]{:S(2)}, u32[]{:S(2)}) collective-permute-start(bf16[256,4608]{1,0:T(8,128)(2,1)} %tokens.7), channel_id=1, source_target_pairs={{0,1},{1,0},{2,3},{3,2},{4,5},{5,4},{6,7},{7,6},{8,9},{9,8},{10,11... | collective-permute-start | bytes 7077896 | tf_op jit(solution)/shard_map/ppermute | solution.py:178
  19.6 11.4 %collective-permute-start.3 = (bf16[256,512]{1,0:T(8,128)(2,1)}, bf16[256,512]{1,0:T(8,128)(2,1)S(1)}, u32[]{:S(2)}, u32[]{:S(2)}) collective-permute-start(bf16[256,512]{1,0:T(8,128)(2,1)} %cot.7), channel_id=1, source_target_pairs={{0,1},{1,0},{2,3},{3,2},{4,5},{5,4},{6,7},{7,6},{8,9},{9,8},{10,11... | collective-permute-start | bytes 786440 | tf_op jit(solution)/shard_map/ppermute | solution.py:179
  23.2 13.7 %copy-start.5 = (bf16[3,128,128]{2,1,0:T(8,128)(2,1)}, bf16[3,128,128]{2,1,0:T(8,128)(2,1)S(1)}, u32[]{:S(2)}) copy-start(bf16[3,128,128]{2,1,0:T(8,128)(2,1)S(1)} %multiply_convert_fusion.own) | copy-start | bytes 294916
  23.2 13.7 %collective-permute-start = (bf16[3,128,128]{2,1,0:T(8,128)(2,1)S(1)}, bf16[3,128,128]{2,1,0:T(8,128)(2,1)S(1)}, u32[]{:S(2)}, u32[]{:S(2)}) collective-permute-start(bf16[3,128,128]{2,1,0:T(8,128)(2,1)S(1)} %multiply_convert_fusion.own), channel_id=1, source_target_pairs={{0,176},{16,0},{32,16},{48,32},{64,48},{80,64},{96,80},{112,96},{1... | collective-permute-start | bytes 294920 | tf_op jit(solution)/shard_map/ppermute | solution.py:183
  28.5 8.4 %collective-permute-start.1 = (bf16[3,128,128]{2,1,0:T(8,128)(2,1)S(1)}, bf16[3,128,128]{2,1,0:T(8,128)(2,1)S(1)}, u32[]{:S(2)}, u32[]{:S(2)}) collective-permute-start(bf16[3,128,128]{2,1,0:T(8,128)(2,1)S(1)} %multiply_convert_fusion.own), channel_id=1, source_target_pairs={{0,16},{16,32},{32,48},{48,64},{64,80},{80,96},{96,112},{112,128},... | collective-permute-start | bytes 294920 | tf_op jit(solution)/shard_map/ppermute | solution.py:182
  31.0 0.7 copy-start.2
  31.7 1.4 %copy-start = (bf16[256,4608]{1,0:T(8,128)(2,1)}, bf16[256,4608]{1,0:T(8,128)(2,1)S(1)}, u32[]{:S(2)}) copy-start(bf16[256,4608]{1,0:T(8,128)(2,1)S(1)} %collective-permute-done.2.theirs) | copy-start | bytes 7077892
  36.8 2.5 %copy-start.1 = (bf16[1152,256]{1,0:T(8,128)(2,1)S(1)}, bf16[1152,256]{1,0:T(8,128)(2,1)}, u32[]{:S(2)}) copy-start(bf16[1152,256]{1,0:T(8,128)(2,1)} %shard_map.102.after) | copy-start | bytes 1769476
  36.8 0.6 copy-start.6
  36.9 0.7 copy-start.7
  39.3 15.1 %collective-permute-start.4 = (bf16[1152,256]{1,0:T(8,128)(2,1)S(1)}, bf16[1152,256]{1,0:T(8,128)(2,1)S(1)}, u32[]{:S(2)}, u32[]{:S(2)}) collective-permute-start(bf16[1152,256]{1,0:T(8,128)(2,1)S(1)} %copy-done.1), channel_id=1, source_target_pairs={{0,192},{1,577},{192,384},{193,1},{384,576},{385,193},{576,0},{577... | collective-permute-start | bytes 1769480 | tf_op jit(solution)/shard_map/ppermute | solution.py:198
  47.4 15.7 %collective-permute-start.5 = (bf16[1152,256]{1,0:T(8,128)(2,1)}, bf16[1152,256]{1,0:T(8,128)(2,1)S(1)}, u32[]{:S(2)}, u32[]{:S(2)}) collective-permute-start(bf16[1152,256]{1,0:T(8,128)(2,1)} %shard_map.105.after), channel_id=1, source_target_pairs={{0,193},{1,576},{192,385},{193,0},{384,577},{385,192},{576,1},{577... | collective-permute-start | bytes 1769480 | tf_op jit(solution)/shard_map/ppermute | solution.py:199
  55.7 3.4 %copy-start.3 = (bf16[1152,256]{1,0:T(8,128)(2,1)}, bf16[1152,256]{1,0:T(8,128)(2,1)S(1)}, u32[]{:S(2)}) copy-start(bf16[1152,256]{1,0:T(8,128)(2,1)S(1)} %add_convert_fusion.1.after) | copy-start | bytes 1769476
  55.8 11.0 %collective-permute-start.6 = (bf16[1152,256]{1,0:T(8,128)(2,1)S(1)}, bf16[1152,256]{1,0:T(8,128)(2,1)S(1)}, u32[]{:S(2)}, u32[]{:S(2)}) collective-permute-start(bf16[1152,256]{1,0:T(8,128)(2,1)S(1)} %add_convert_fusion.1.after), channel_id=1, source_target_pairs={{0,192},{1,577},{192,384},{193,1},{384,576},{385,193},{576,0},{577... | collective-permute-start | bytes 1769480 | tf_op jit(solution)/shard_map/ppermute | solution.py:202
  68.3 9.2 %collective-permute-start.7 = (bf16[4,96,256]{2,1,0:T(8,128)(2,1)S(1)}, bf16[4,96,256]{2,1,0:T(8,128)(2,1)S(1)}, u32[]{:S(2)}, u32[]{:S(2)}) collective-permute-start(bf16[4,96,256]{2,1,0:T(8,128)(2,1)S(1)} %get-tuple-element.10), channel_id=1, source_target_pairs={{0,16},{16,32},{32,48},{48,64},{64,80},{80,96},{96,112},{112,128},... | collective-permute-start | bytes 589832 | tf_op jit(solution)/shard_map/ppermute | solution.py:211
  70.2 8.1 %collective-permute-start.8 = (bf16[4,96,256]{2,1,0:T(8,128)(2,1)S(1)}, bf16[4,96,256]{2,1,0:T(8,128)(2,1)S(1)}, u32[]{:S(2)}, u32[]{:S(2)}) collective-permute-start(bf16[4,96,256]{2,1,0:T(8,128)(2,1)S(1)} %get-tuple-element.11), channel_id=1, source_target_pairs={{0,176},{16,0},{32,16},{48,32},{64,48},{80,64},{96,80},{112,96},{1... | collective-permute-start | bytes 589832 | tf_op jit(solution)/shard_map/ppermute | solution.py:212
  79.2 29.2 %all-to-all-start = ((bf16[64,6,256]{2,1,0:T(8,128)(2,1)}), bf16[64,6,256]{2,1,0:T(8,128)(2,1)S(1)}, u32[]{:S(2)}, u32[]{:S(2)}) async-start(bf16[64,6,256]{2,1,0:T(8,128)(2,1)} %reshape.24), calls=%async_computation | async-start | bytes 524288 | tf_op jit(solution)/shard_map/all_to_all | solution.py:215
  108.3 0.7 copy-start.4
Sparse Core Ops, SparseCore 0:
  39.4 45.8 all-gather.2

commit v5 on v4

--- a/solution.py
+++ b/solution.py
@@ -112,6 +112,7 @@
         out_shape=(shape, shape, shape),
         in_specs=[vmem] * 4 + [pl.BlockSpec(memory_space=pl.ANY)],
         out_specs=(vmem, vmem, vmem),
+        compiler_params=pltpu.CompilerParams(vmem_limit_bytes=60 * 2**20),
         cost_estimate=pl.CostEstimate(flops=20 * master.size, bytes_accessed=24 * master.size + 2 * terms.size, transcendentals=0),
     )(terms, master, first, second, after)
 

time: 119 us -> 119 us (level)
  no operation moved by 1% of the time
where the time goes in v5:
time: 119 us; the launch traced here: 118 us
  starting transfers between devices  53 us (45%)
  Pallas kernels  24.2 us (20%)
  waiting for transfers between devices  16.6 us (14%)
  between operations  14.3 us (12%)
  other arithmetic  5.03 us (4%)
  local copies, waits for them, and re-layouts  4.38 us (4%)
    pallas_call x4, Pallas kernels, terms(): pl.pallas_call(functools.partial(term_kernel, plan), out_shape=[jax.Shape...  15.2 us
    all_to_all x1, starting transfers between devices, local(): last = lax.all_to_all(last, ('zh', 'y', 'c'), 0, 0, tiled=True)  13.8 us
    ppermute x1, starting transfers between devices, local(): theirs = lax.ppermute(tokens, 'c', swap)  12.4 us
    all_to_all x1, waiting for transfers between devices, local(): last = lax.all_to_all(last, ('zh', 'y', 'c'), 0, 0, tiled=True)  9.68 us
    pallas_call x1, Pallas kernels, project(): pl.pallas_call(project_kernel, out_shape=jax.ShapeDtypeStruct((rows, colu...  5.67 us
    ppermute x1, starting transfers between devices, local(): above = lax.ppermute(w, ('zh', 'zl'), z_down)  5.29 us
    ppermute x1, starting transfers between devices, local(): down = lax.ppermute(third(zl + 2), ('zh', 'zl'), z_down)  4.88 us
    ppermute x1, starting transfers between devices, local(): two_on = lax.ppermute(two_on, ('x', 'c'), straight)  4.39 us
  transfers between devices with their start and end apart: 11, of which 4 were waited for; matrix products, arithmetic and copies ran while one was open for 5% of the time, Pallas kernels for 18%

profile of v5, /device:TPU:1, one launch (start us, length us, event | category | flops | bytes accessed | tf_op | source)
XLA Modules:
  0.0 117.6 jit_solution(9025027522560517774)
XLA Ops:
  7.2 12.4 %collective-permute-start.2 = (bf16[256,4608]{1,0:T(8,128)(2,1)}, bf16[256,4608]{1,0:T(8,128)(2,1)S(1)}, u32[]{:S(2)}, u32[]{:S(2)}) collective-permute-start(bf16[256,4608]{1,0:T(8,128)(2,1)} %tokens.7), channel_id=1, source_target_pairs={{0,1},{1,0},{2,3},{3,2},{4,5},{5,4},{6,7},{7,6},{8,9},{9,8},{10,11... | collective-permute-start | bytes 7077896 | tf_op jit(solution)/shard_map/ppermute | solution.py:179
  19.6 1.9 %collective-permute-start.3 = (bf16[256,512]{1,0:T(8,128)(2,1)}, bf16[256,512]{1,0:T(8,128)(2,1)S(1)}, u32[]{:S(2)}, u32[]{:S(2)}) collective-permute-start(bf16[256,512]{1,0:T(8,128)(2,1)} %cot.7), channel_id=1, source_target_pairs={{0,1},{1,0},{2,3},{3,2},{4,5},{5,4},{6,7},{7,6},{8,9},{9,8},{10,11... | collective-permute-start | bytes 786440 | tf_op jit(solution)/shard_map/ppermute | solution.py:180
  21.6 0.7 bitcast_convert_fusion
  22.3 0.9 multiply_convert_fusion.own
  23.2 5.3 %collective-permute-start = (bf16[3,128,128]{2,1,0:T(8,128)(2,1)S(1)}, bf16[3,128,128]{2,1,0:T(8,128)(2,1)S(1)}, u32[]{:S(2)}, u32[]{:S(2)}) collective-permute-start(bf16[3,128,128]{2,1,0:T(8,128)(2,1)S(1)} %multiply_convert_fusion.own), channel_id=1, source_target_pairs={{0,176},{16,0},{32,16},{48,32},{64,48},{80,64},{96,80},{112,96},{1... | collective-permute-start | bytes 294920 | tf_op jit(solution)/shard_map/ppermute | solution.py:184
  28.5 1.9 %collective-permute-start.1 = (bf16[3,128,128]{2,1,0:T(8,128)(2,1)S(1)}, bf16[3,128,128]{2,1,0:T(8,128)(2,1)S(1)}, u32[]{:S(2)}, u32[]{:S(2)}) collective-permute-start(bf16[3,128,128]{2,1,0:T(8,128)(2,1)S(1)} %multiply_convert_fusion.own), channel_id=1, source_target_pairs={{0,16},{16,32},{32,48},{48,64},{64,80},{80,96},{96,112},{112,128},... | collective-permute-start | bytes 294920 | tf_op jit(solution)/shard_map/ppermute | solution.py:183
  30.4 0.1 stack.23
  30.5 0.5 convert_element_type.58.where
  31.0 0.7 copy-done.2
  31.7 1.4 %copy-done = bf16[256,4608]{1,0:T(8,128)(2,1)} copy-done((bf16[256,4608]{1,0:T(8,128)(2,1)}, bf16[256,4608]{1,0:T(8,128)(2,1)S(1)}, u32[]{:S(2)}) %copy-start) | copy-done | bytes 2359320
  33.2 3.6 %shard_map.102.after = bf16[1152,256]{1,0:T(8,128)(2,1)} custom-call(s32[5]{0:T(128)} %convert_element_type.58.where, bf16[256,4608]{1,0:T(8,128)(2,1)} %tokens.7, bf16[256,4608]{1,0:T(8,128)(2,1)} %copy-done, bf16[256,512]{1,0:T(8,128)(2,1)} %cot.7, bf16[256,512]{1,0:T(8,128)(2,1)} %copy-done.2, bf16[256,512]{1,0:T(8,128)(2,1)} %cot.7), custom_call_target="tpu_custom_call" | custom-call | flops 301989888 | bytes 1179648 | tf_op jit(solution)/shard_map/pallas_call | solution.py:154
  36.9 0.6 copy-done.6
  37.5 1.7 %shard_map.103 = bf16[9,128,128]{2,1,0:T(8,128)(2,1)} custom-call(s32[1]{0:T(128)} %bitcast.zl_ref, bf16[3,128,128]{2,1,0:T(8,128)(2,1)} %copy-done.5, bf16[3,128,128]{2,1,0:T(8,128)(2,1)} %copy-done.6, bf16[3,128,128]{2,1,0:T(8,128)(2,1)} %copy-done.7, bf16[1152,256]{1,0:T(8,128)(2,1)} %shard_map.102.after), custom_call_target="tpu_custom_call" | custom-call | bytes 589824 | tf_op jit(solution)/shard_map/pallas_call | solution.py:82
  39.3 4.4 %collective-permute-start.4 = (bf16[1152,256]{1,0:T(8,128)(2,1)S(1)}, bf16[1152,256]{1,0:T(8,128)(2,1)S(1)}, u32[]{:S(2)}, u32[]{:S(2)}) collective-permute-start(bf16[1152,256]{1,0:T(8,128)(2,1)S(1)} %copy-done.1), channel_id=1, source_target_pairs={{0,192},{1,577},{192,384},{193,1},{384,576},{385,193},{576,0},{577... | collective-permute-start | bytes 1769480 | tf_op jit(solution)/shard_map/ppermute | solution.py:199
  43.7 3.7 %shard_map.105.after = bf16[1152,256]{1,0:T(8,128)(2,1)} custom-call(s32[5]{0:T(128)} %convert_element_type.58.where, bf16[256,4608]{1,0:T(8,128)(2,1)} %tokens.7, bf16[256,4608]{1,0:T(8,128)(2,1)} %copy-done, bf16[256,512]{1,0:T(8,128)(2,1)} %cot.7, bf16[256,512]{1,0:T(8,128)(2,1)} %copy-done.2, bf16[1152,256]{1,0:T(8,128)(2,1)} %shard_map.102.after), custom_call_target="tpu_custom_call" | custom-call | flops 301989888 | bytes 1179648 | tf_op jit(solution)/shard_map/pallas_call | solution.py:154
  47.4 3.1 %collective-permute-start.5 = (bf16[1152,256]{1,0:T(8,128)(2,1)}, bf16[1152,256]{1,0:T(8,128)(2,1)S(1)}, u32[]{:S(2)}, u32[]{:S(2)}) collective-permute-start(bf16[1152,256]{1,0:T(8,128)(2,1)} %shard_map.105.after), channel_id=1, source_target_pairs={{0,193},{1,576},{192,385},{193,0},{384,577},{385,192},{576,1},{577... | collective-permute-start | bytes 1769480 | tf_op jit(solution)/shard_map/ppermute | solution.py:200
  50.4 3.9 %shard_map.106 = f32[1152,256]{1,0:T(8,128)} custom-call(s32[5]{0:T(128)} %convert_element_type.58.where, bf16[256,4608]{1,0:T(8,128)(2,1)} %tokens.7, bf16[256,4608]{1,0:T(8,128)(2,1)} %copy-done, bf16[256,512]{1,0:T(8,128)(2,1)} %cot.7, bf16[256,512]{1,0:T(8,128)(2,1)} %copy-done.2, bf16[1152,256]{1,0:T(8,128)(2,1)} %shard_map.105.after), custom_call_target="tpu_custom_call" | custom-call | flops 301989888 | bytes 1179648 | tf_op jit(solution)/shard_map/pallas_call | solution.py:154
  54.3 1.4 %add_convert_fusion.1.after = bf16[1152,256]{1,0:T(8,128)(2,1)S(1)} fusion(f32[1152,256]{1,0:T(8,128)} %shard_map.106, bf16[1152,256]{1,0:T(8,128)(2,1)S(1)} %collective-permute-done.4), kind=kLoop, calls=%fused_computation.1 | loop fusion | flops 884736 | bytes 2359296 | tf_op jit(solution)/shard_map/convert_element_type | solution.py:201
  55.8 3.4 %collective-permute-start.6 = (bf16[1152,256]{1,0:T(8,128)(2,1)S(1)}, bf16[1152,256]{1,0:T(8,128)(2,1)S(1)}, u32[]{:S(2)}, u32[]{:S(2)}) collective-permute-start(bf16[1152,256]{1,0:T(8,128)(2,1)S(1)} %add_convert_fusion.1.after), channel_id=1, source_target_pairs={{0,192},{1,577},{192,384},{193,1},{384,576},{385,193},{576,0},{577... | collective-permute-start | bytes 1769480 | tf_op jit(solution)/shard_map/ppermute | solution.py:203
  59.2 3.9 %shard_map.107 = f32[1152,256]{1,0:T(8,128)} custom-call(s32[5]{0:T(128)} %convert_element_type.58.where, bf16[256,4608]{1,0:T(8,128)(2,1)} %tokens.7, bf16[256,4608]{1,0:T(8,128)(2,1)} %copy-done, bf16[256,512]{1,0:T(8,128)(2,1)} %cot.7, bf16[256,512]{1,0:T(8,128)(2,1)} %copy-done.2, bf16[1152,256]{1,0:T(8,128)(2,1)} %copy-done.3), custom_call_target="tpu_custom_call" | custom-call | flops 301989888 | bytes 1179648 | tf_op jit(solution)/shard_map/pallas_call | solution.py:154
  63.1 3.7 %collective-permute-done.6 = bf16[1152,256]{1,0:T(8,128)(2,1)S(1)} collective-permute-done((bf16[1152,256]{1,0:T(8,128)(2,1)S(1)}, bf16[1152,256]{1,0:T(8,128)(2,1)S(1)}, u32[]{:S(2)}, u32[]{:S(2)}) %collective-permute-start.6) | collective-permute-done | bytes 589856 | tf_op jit(solution)/shard_map/ppermute | solution.py:203
  66.8 1.4 %add_convert_fusion = bf16[1152,256]{1,0:T(8,128)(2,1)S(1)} fusion(bf16[1152,256]{1,0:T(8,128)(2,1)S(1)} %collective-permute-done.6, f32[1152,256]{1,0:T(8,128)} %shard_map.107, bf16[1152,256]{1,0:T(8,128)(2,1)S(1)} %collective-permute-done.5), kind=kLoop, calls=%fused_computation | loop fusion | flops 1474560 | bytes 2949120 | tf_op jit(solution)/shard_map/convert_element_type | solution.py:204
  68.3 1.9 %collective-permute-start.7 = (bf16[4,96,256]{2,1,0:T(8,128)(2,1)S(1)}, bf16[4,96,256]{2,1,0:T(8,128)(2,1)S(1)}, u32[]{:S(2)}, u32[]{:S(2)}) collective-permute-start(bf16[4,96,256]{2,1,0:T(8,128)(2,1)S(1)} %get-tuple-element.10), channel_id=1, source_target_pairs={{0,16},{16,32},{32,48},{48,64},{64,80},{80,96},{96,112},{112,128},... | collective-permute-start | bytes 589832 | tf_op jit(solution)/shard_map/ppermute | solution.py:212
  70.2 4.9 %collective-permute-start.8 = (bf16[4,96,256]{2,1,0:T(8,128)(2,1)S(1)}, bf16[4,96,256]{2,1,0:T(8,128)(2,1)S(1)}, u32[]{:S(2)}, u32[]{:S(2)}) collective-permute-start(bf16[4,96,256]{2,1,0:T(8,128)(2,1)S(1)} %get-tuple-element.11), channel_id=1, source_target_pairs={{0,176},{16,0},{32,16},{48,32},{64,48},{80,64},{96,80},{112,96},{1... | collective-permute-start | bytes 589832 | tf_op jit(solution)/shard_map/ppermute | solution.py:213
  75.1 2.3 %collective-permute-done.7 = bf16[4,96,256]{2,1,0:T(8,128)(2,1)S(1)} collective-permute-done((bf16[4,96,256]{2,1,0:T(8,128)(2,1)S(1)}, bf16[4,96,256]{2,1,0:T(8,128)(2,1)S(1)}, u32[]{:S(2)}, u32[]{:S(2)}) %collective-permute-start.7) | collective-permute-done | bytes 196640 | tf_op jit(solution)/shard_map/ppermute | solution.py:212
  77.4 0.9 collective-permute-done.8
  78.4 0.8 reshape.24
  79.2 13.8 %all-to-all-start = ((bf16[64,6,256]{2,1,0:T(8,128)(2,1)}), bf16[64,6,256]{2,1,0:T(8,128)(2,1)S(1)}, u32[]{:S(2)}, u32[]{:S(2)}) async-start(bf16[64,6,256]{2,1,0:T(8,128)(2,1)} %reshape.24), calls=%async_computation | async-start | bytes 524288 | tf_op jit(solution)/shard_map/all_to_all | solution.py:216
  93.0 5.7 %shard_map.104.after = bf16[256,512]{1,0:T(8,128)(2,1)} custom-call(bf16[256,4608]{1,0:T(8,128)(2,1)} %tokens.7, bf16[16,9,128,128]{3,2,1,0:T(8,128)(2,1)} %bitcast.21), custom_call_target="tpu_custom_call" | custom-call | flops 1207959552 | bytes 7077888 | tf_op jit(solution)/shard_map/pallas_call | solution.py:54
  98.7 9.7 %all-to-all-done = bf16[64,6,256]{2,1,0:T(8,128)(2,1)S(1)} async-done(((bf16[64,6,256]{2,1,0:T(8,128)(2,1)}), bf16[64,6,256]{2,1,0:T(8,128)(2,1)S(1)}, u32[]{:S(2)}, u32[]{:S(2)}) %all-to-all-start) | async-done | bytes 196640 | tf_op jit(solution)/shard_map/all_to_all | solution.py:216
  108.3 0.7 copy-done.4
  109.0 1.7 %shard_map.108 = (f32[6,512]{1,0:T(8,128)}, f32[6,512]{1,0:T(8,128)}, f32[6,512]{1,0:T(8,128)}) custom-call(bf16[32,2,6,256]{3,2,1,0:T(8,128)(2,1)} %bitcast.24, f32[6,512]{1,0:T(8,128)} %master.1, f32[6,512]{1,0:T(8,128)} %first.1, f32[6,512]{1,0:T(8,128)} %second.1, bf16[256,512]{1,0:T(8,128)(2,1)} %shard_map.104.after), custom_call_target="tpu_custom_call" | custom-call | flops 61440 | bytes 270336 | tf_op jit(solution)/shard_map/pallas_call | solution.py:110
  (23 shorter events, 0.3 us)
Async XLA Ops:
  7.2 85.8 %all-gather.3.cloned.1.call-start = ((), (), s32[]{:S(2)}) async-start(), calls=%async_computation.1 | async-start | bytes 5013504 | tf_op jit(solution)/shard_map/all_gather | solution.py:196
  7.2 23.8 %collective-permute-start.2 = (bf16[256,4608]{1,0:T(8,128)(2,1)}, bf16[256,4608]{1,0:T(8,128)(2,1)S(1)}, u32[]{:S(2)}, u32[]{:S(2)}) collective-permute-start(bf16[256,4608]{1,0:T(8,128)(2,1)} %tokens.7), channel_id=1, source_target_pairs={{0,1},{1,0},{2,3},{3,2},{4,5},{5,4},{6,7},{7,6},{8,9},{9,8},{10,11... | collective-permute-start | bytes 7077896 | tf_op jit(solution)/shard_map/ppermute | solution.py:179
  19.6 11.4 %collective-permute-start.3 = (bf16[256,512]{1,0:T(8,128)(2,1)}, bf16[256,512]{1,0:T(8,128)(2,1)S(1)}, u32[]{:S(2)}, u32[]{:S(2)}) collective-permute-start(bf16[256,512]{1,0:T(8,128)(2,1)} %cot.7), channel_id=1, source_target_pairs={{0,1},{1,0},{2,3},{3,2},{4,5},{5,4},{6,7},{7,6},{8,9},{9,8},{10,11... | collective-permute-start | bytes 786440 | tf_op jit(solution)/shard_map/ppermute | solution.py:180
  23.2 13.7 %copy-start.5 = (bf16[3,128,128]{2,1,0:T(8,128)(2,1)}, bf16[3,128,128]{2,1,0:T(8,128)(2,1)S(1)}, u32[]{:S(2)}) copy-start(bf16[3,128,128]{2,1,0:T(8,128)(2,1)S(1)} %multiply_convert_fusion.own) | copy-start | bytes 294916
  23.2 13.7 %collective-permute-start = (bf16[3,128,128]{2,1,0:T(8,128)(2,1)S(1)}, bf16[3,128,128]{2,1,0:T(8,128)(2,1)S(1)}, u32[]{:S(2)}, u32[]{:S(2)}) collective-permute-start(bf16[3,128,128]{2,1,0:T(8,128)(2,1)S(1)} %multiply_convert_fusion.own), channel_id=1, source_target_pairs={{0,176},{16,0},{32,16},{48,32},{64,48},{80,64},{96,80},{112,96},{1... | collective-permute-start | bytes 294920 | tf_op jit(solution)/shard_map/ppermute | solution.py:184
  28.5 8.4 %collective-permute-start.1 = (bf16[3,128,128]{2,1,0:T(8,128)(2,1)S(1)}, bf16[3,128,128]{2,1,0:T(8,128)(2,1)S(1)}, u32[]{:S(2)}, u32[]{:S(2)}) collective-permute-start(bf16[3,128,128]{2,1,0:T(8,128)(2,1)S(1)} %multiply_convert_fusion.own), channel_id=1, source_target_pairs={{0,16},{16,32},{32,48},{48,64},{64,80},{80,96},{96,112},{112,128},... | collective-permute-start | bytes 294920 | tf_op jit(solution)/shard_map/ppermute | solution.py:183
  31.0 0.7 copy-start.2
  31.7 1.4 %copy-start = (bf16[256,4608]{1,0:T(8,128)(2,1)}, bf16[256,4608]{1,0:T(8,128)(2,1)S(1)}, u32[]{:S(2)}) copy-start(bf16[256,4608]{1,0:T(8,128)(2,1)S(1)} %collective-permute-done.2.theirs) | copy-start | bytes 7077892
  36.8 2.5 %copy-start.1 = (bf16[1152,256]{1,0:T(8,128)(2,1)S(1)}, bf16[1152,256]{1,0:T(8,128)(2,1)}, u32[]{:S(2)}) copy-start(bf16[1152,256]{1,0:T(8,128)(2,1)} %shard_map.102.after) | copy-start | bytes 1769476
  36.8 0.6 copy-start.6
  36.9 0.7 copy-start.7
  39.3 15.1 %collective-permute-start.4 = (bf16[1152,256]{1,0:T(8,128)(2,1)S(1)}, bf16[1152,256]{1,0:T(8,128)(2,1)S(1)}, u32[]{:S(2)}, u32[]{:S(2)}) collective-permute-start(bf16[1152,256]{1,0:T(8,128)(2,1)S(1)} %copy-done.1), channel_id=1, source_target_pairs={{0,192},{1,577},{192,384},{193,1},{384,576},{385,193},{576,0},{577... | collective-permute-start | bytes 1769480 | tf_op jit(solution)/shard_map/ppermute | solution.py:199
  47.4 15.7 %collective-permute-start.5 = (bf16[1152,256]{1,0:T(8,128)(2,1)}, bf16[1152,256]{1,0:T(8,128)(2,1)S(1)}, u32[]{:S(2)}, u32[]{:S(2)}) collective-permute-start(bf16[1152,256]{1,0:T(8,128)(2,1)} %shard_map.105.after), channel_id=1, source_target_pairs={{0,193},{1,576},{192,385},{193,0},{384,577},{385,192},{576,1},{577... | collective-permute-start | bytes 1769480 | tf_op jit(solution)/shard_map/ppermute | solution.py:200
  55.7 3.4 %copy-start.3 = (bf16[1152,256]{1,0:T(8,128)(2,1)}, bf16[1152,256]{1,0:T(8,128)(2,1)S(1)}, u32[]{:S(2)}) copy-start(bf16[1152,256]{1,0:T(8,128)(2,1)S(1)} %add_convert_fusion.1.after) | copy-start | bytes 1769476
  55.8 11.0 %collective-permute-start.6 = (bf16[1152,256]{1,0:T(8,128)(2,1)S(1)}, bf16[1152,256]{1,0:T(8,128)(2,1)S(1)}, u32[]{:S(2)}, u32[]{:S(2)}) collective-permute-start(bf16[1152,256]{1,0:T(8,128)(2,1)S(1)} %add_convert_fusion.1.after), channel_id=1, source_target_pairs={{0,192},{1,577},{192,384},{193,1},{384,576},{385,193},{576,0},{577... | collective-permute-start | bytes 1769480 | tf_op jit(solution)/shard_map/ppermute | solution.py:203
  68.3 9.2 %collective-permute-start.7 = (bf16[4,96,256]{2,1,0:T(8,128)(2,1)S(1)}, bf16[4,96,256]{2,1,0:T(8,128)(2,1)S(1)}, u32[]{:S(2)}, u32[]{:S(2)}) collective-permute-start(bf16[4,96,256]{2,1,0:T(8,128)(2,1)S(1)} %get-tuple-element.10), channel_id=1, source_target_pairs={{0,16},{16,32},{32,48},{48,64},{64,80},{80,96},{96,112},{112,128},... | collective-permute-start | bytes 589832 | tf_op jit(solution)/shard_map/ppermute | solution.py:212
  70.2 8.1 %collective-permute-start.8 = (bf16[4,96,256]{2,1,0:T(8,128)(2,1)S(1)}, bf16[4,96,256]{2,1,0:T(8,128)(2,1)S(1)}, u32[]{:S(2)}, u32[]{:S(2)}) collective-permute-start(bf16[4,96,256]{2,1,0:T(8,128)(2,1)S(1)} %get-tuple-element.11), channel_id=1, source_target_pairs={{0,176},{16,0},{32,16},{48,32},{64,48},{80,64},{96,80},{112,96},{1... | collective-permute-start | bytes 589832 | tf_op jit(solution)/shard_map/ppermute | solution.py:213
  79.2 29.2 %all-to-all-start = ((bf16[64,6,256]{2,1,0:T(8,128)(2,1)}), bf16[64,6,256]{2,1,0:T(8,128)(2,1)S(1)}, u32[]{:S(2)}, u32[]{:S(2)}) async-start(bf16[64,6,256]{2,1,0:T(8,128)(2,1)} %reshape.24), calls=%async_computation | async-start | bytes 524288 | tf_op jit(solution)/shard_map/all_to_all | solution.py:216
  108.3 0.7 copy-start.4
Sparse Core Ops, SparseCore 0:
  39.4 45.8 all-gather.2
